TPU v7x, 256 devices: a whole 4x4x8 slice. The times are simulated.
256 devices in a mesh: row: 8 (over x, core), col: 32 (over z, y).
Axes of the slice: x: 4, y: 4, z: 8, core: 2. Of those that a mesh axis runs over, the one named last changes fastest.
Arguments:
- density: float32 [1024, 8, 128, 128], P(('row', 'col'))
- pattern: int32 [1024, 8], P(('row', 'col')), may hold values from -1 to 1023, as said below
- square_target: int32 [1024, 16], P(('row', 'col')), may hold values from -1 to 1023, as said below
- cube_target: int32 [1024, 24], P(('row', 'col')), may hold values from -1 to 1023, as said below
Outputs:
- squared: float32 [1024, 16, 128, 128], P(('row', 'col'))
- purified: float32 [1024, 24, 128, 128], P(('row', 'col'))
Inputs may be any that keep to these rules, and one draw needn't show every extreme that they name: `pattern`: in each block row the live slots come first and slot 0 holds the row's own block column; live columns are distinct and lie within 4 of the row's index, counted around the ends; each row has 5 to 8 live slots, and some row has exactly 8, some exactly 5. `square_target`: as pattern, with columns within 8 of the row's index and 5 to 16 live slots, both reached. `cube_target`: as pattern, with columns within 12 of the row's index and 5 to 24 live slots, both reached.
All inputs are finite; a program needn't handle non-finite values.
Results may differ from a plain program's by a relative error of at most 0.0003.
Values sent between devices are 32-bit elements; how exact they have to be, the bound alone decides.
No kernel may reach another device: no remote copies, remote signals or barrier semaphores. Data moves between devices by JAX's collectives and lax.ppermute only.
A program may use at most 192 MiB of HBM per device.

v0:
```python
import jax
import jax.numpy as jnp
from jax import lax
from jax.sharding import PartitionSpec as P

H = 4


EXACT_ARITHMETIC = lax.Precision.HIGHEST


def passed_along(block, axis, distance):
    devices = range(lax.axis_size(axis))
    route = [((i - distance) % len(devices), i) for i in devices]
    return lax.ppermute(block, axis, route)


def block_product(
    left_blocks, left_cols, right_blocks, right_column_ids, targets, row_base, row_total
):

    def one_row(row_item):
        blocks, columns, target_row = row_item
        slot_rows = jnp.where(columns >= 0, jnp.mod(columns - row_base, row_total), 0)
        selected_entries = jnp.take(right_blocks, slot_rows, axis=0)
        picked_cols = jnp.take(right_column_ids, slot_rows, axis=0)
        block_products_list = jnp.einsum(
            "sab,subc->suac",
            blocks,
            selected_entries,
            precision=EXACT_ARITHMETIC,
            preferred_element_type=jnp.float32,
        )
        matching_entries = jnp.logical_and(
            picked_cols[None, :, :] == target_row[:, None, None], target_row[:, None, None] >= 0
        ).astype(jnp.float32)
        return jnp.einsum(
            "fpn,pngi->fgi",
            matching_entries,
            block_products_list,
            precision=EXACT_ARITHMETIC,
            preferred_element_type=jnp.float32,
        )

    return lax.map(one_row, (left_blocks, left_cols, targets))


def combine(squared, square_target, cubed, cube_target):
    shared_slots = jnp.logical_and(
        cube_target[:, :, None] == square_target[:, None, :], cube_target[:, :, None] >= 0
    ).astype(jnp.float32)
    carried = jnp.einsum(
        "rts,rsab->rtab",
        shared_slots,
        squared,
        precision=EXACT_ARITHMETIC,
        preferred_element_type=jnp.float32,
    )
    kept_slots = (cube_target >= 0).astype(jnp.float32)[:, :, None, None]
    return kept_slots * (3.0 * carried - 2.0 * cubed)


def gather_rim(pieces, from_below, from_above):
    below_list = [from_below(tuple((member for member in pieces)), 1)]
    above_list = [from_above(tuple((member for member in pieces)), 1)]
    joined = []
    for member_index in range(len(pieces)):
        stacked = (
            [got[member_index] for got in reversed(below_list)]
            + [pieces[member_index]]
            + [got[member_index] for got in above_list]
        )
        joined.append(jnp.concatenate(stacked, axis=0))
    return tuple(joined)


def local(density, pattern, square_target, cube_target):
    row_count = density.shape[0]
    row_total = row_count * lax.axis_size(("row", "col"))
    first_row = lax.axis_index(("row", "col")) * row_count
    live_slots = (pattern >= 0)[:, :, None, None]
    masked = jnp.where(live_slots, density, jnp.zeros_like(density))

    def density_lower(payload, distance):
        return passed_along(payload, ("row", "col"), distance)

    def density_upper(payload, distance):
        return passed_along(payload, ("row", "col"), -distance)

    near_blocks, near_cols = gather_rim((masked, pattern), density_lower, density_upper)
    squared = block_product(
        masked, pattern, near_blocks, near_cols, square_target, first_row - H, row_total
    )

    def square_lower(payload, distance):
        return passed_along(payload, ("row", "col"), distance)

    def square_upper(payload, distance):
        return passed_along(payload, ("row", "col"), -distance)

    rim_blocks, rim_cols = gather_rim((squared, square_target), square_lower, square_upper)
    cubed = block_product(
        masked, pattern, rim_blocks, rim_cols, cube_target, first_row - H, row_total
    )
    return (squared, combine(squared, square_target, cubed, cube_target))


def solution(mesh):
    in_specs = (
        P(("row", "col"), None, None, None),
        P(("row", "col"), None),
        P(("row", "col"), None),
        P(("row", "col"), None),
    )
    out_specs = (P(("row", "col"), None, None, None), P(("row", "col"), None, None, None))
    return jax.shard_map(local, mesh=mesh, in_specs=in_specs, out_specs=out_specs, check_vma=False)
```

profile of v0, /device:TPU:0, one launch (start us, length us, event | category | flops | bytes accessed | tf_op | source)
XLA Modules:
  0.0 467.2 jit_solution(9771911244978256445)
XLA Ops:
  3.2 8.3 %collective-permute-start.3 = (f32[4,8,128,128]{3,2,1,0:T(8,128)S(1)}, f32[4,8,128,128]{3,2,1,0:T(8,128)}, u32[]{:S(2)}, u32[]{:S(2)}) collective-permute-start(f32[4,8,128,128]{3,2,1,0:T(8,128)S(1)} %broadcast_select_fusion.2), channel_id=1, source_target_pairs={{1,0},{2,1},{3,2},{4,3},{5,4},{6,5},{7,6},{8,7},{9,8},{10,9},{11,1... | collective-permute-start | bytes 6291464 | tf_op jit(solution)/shard_map/ppermute | solution.py:15
  11.5 7.2 %collective-permute-start.1 = (s32[4,8]{1,0:T(4,128)}, s32[4,8]{1,0:T(4,128)S(1)}, u32[]{:S(2)}, u32[]{:S(2)}) collective-permute-start(s32[4,8]{1,0:T(4,128)} %param.9), channel_id=1, source_target_pairs={{1,0},{2,1},{3,2},{4,3},{5,4},{6,5},{7,6},{8,7},{9,8},{10,9},{11,1... | collective-permute-start | bytes 392 | tf_op jit(solution)/shard_map/ppermute | solution.py:15
  18.7 38.4 %collective-permute-done = s32[4,8]{1,0:T(4,128)S(1)} collective-permute-done((s32[4,8]{1,0:T(4,128)}, s32[4,8]{1,0:T(4,128)S(1)}, u32[]{:S(2)}, u32[]{:S(2)}) %collective-permute-start) | collective-permute-done | bytes 160 | tf_op jit(solution)/shard_map/ppermute | solution.py:15
  63.4 105.5 %while.24 = (s32[]{:T(128)}, f32[4,16,128,128]{3,1,2,0:T(8,128)}, s32[4,8]{1,0:T(4,128)S(1)}, s32[]{:T(128)}, s32[12,8]{1,0:T(8,128)S(1)}, /*index=5*/s32[4,16]{...) while((s32[]{:T(128)}, f32[4,16,128,128]{3,1,2,0:T(8,128)}, ...), condition=%wide.region_1.2_spmd, body=%wide.region_0.1_spmd.sunk | while | flops 1812991232 | bytes 30940452 | solution.py:45
  63.4 5.6 %gather_fusion = f32[8,8,128,128]{3,2,1,0:T(8,128)} fusion(f32[12,8,128,128]{3,2,1,0:T(8,128)} %get-tuple-element.378, s32[1024]{0:T(1024)S(1)} %pad_clamp_fusion.4), kind=kCustom, calls=%fused_computation.1.clone.1 | custom fusion | bytes 8388640 | tf_op jit(solution)/shard_map/while/body/eval_jaxpr/jit(_take)/gather | solution.py:25
  69.0 9.9 %fusion.77 = f32[8,8,128,128]{3,2,1,0:T(8,128)} fusion(f32[8,8,128,128]{3,2,1,0:T(8,128)} %gather_fusion, pred[8]{0:T(512)(128)(4,1)S(1)} %compare_and_fusion.4, f32[4,8,128,128]{3,2,1,0:T(8,128)S(1)} %get-tuple-element.379, s32[]{:T(128)} %get-tuple-element.363), kind=kOutput, calls=%fused_computation.6.clone.1 | convolution fusion | flops 1611661312 | bytes 8913412 | tf_op jit(solution)/shard_map/while/body/eval_jaxpr/sab,subc->suac/dot_general | solution.py:27
  95.4 9.9 %fusion.77 = f32[8,8,128,128]{3,2,1,0:T(8,128)} fusion(f32[8,8,128,128]{3,2,1,0:T(8,128)} %gather_fusion, pred[8]{0:T(512)(128)(4,1)S(1)} %compare_and_fusion.4, f32[4,8,128,128]{3,2,1,0:T(8,128)S(1)} %get-tuple-element.379, s32[]{:T(128)} %get-tuple-element.363), kind=kOutput, calls=%fused_computation.6.clone.1 | convolution fusion | flops 1611661312 | bytes 8913412 | tf_op jit(solution)/shard_map/while/body/eval_jaxpr/sab,subc->suac/dot_general | solution.py:27
  116.2 5.6 %gather_fusion = f32[8,8,128,128]{3,2,1,0:T(8,128)} fusion(f32[12,8,128,128]{3,2,1,0:T(8,128)} %get-tuple-element.378, s32[1024]{0:T(1024)S(1)} %pad_clamp_fusion.4), kind=kCustom, calls=%fused_computation.1.clone.1 | custom fusion | bytes 8388640 | tf_op jit(solution)/shard_map/while/body/eval_jaxpr/jit(_take)/gather | solution.py:25
  121.8 9.9 %fusion.77 = f32[8,8,128,128]{3,2,1,0:T(8,128)} fusion(f32[8,8,128,128]{3,2,1,0:T(8,128)} %gather_fusion, pred[8]{0:T(512)(128)(4,1)S(1)} %compare_and_fusion.4, f32[4,8,128,128]{3,2,1,0:T(8,128)S(1)} %get-tuple-element.379, s32[]{:T(128)} %get-tuple-element.363), kind=kOutput, calls=%fused_computation.6.clone.1 | convolution fusion | flops 1611661312 | bytes 8913412 | tf_op jit(solution)/shard_map/while/body/eval_jaxpr/sab,subc->suac/dot_general | solution.py:27
  148.2 9.9 %fusion.77 = f32[8,8,128,128]{3,2,1,0:T(8,128)} fusion(f32[8,8,128,128]{3,2,1,0:T(8,128)} %gather_fusion, pred[8]{0:T(512)(128)(4,1)S(1)} %compare_and_fusion.4, f32[4,8,128,128]{3,2,1,0:T(8,128)S(1)} %get-tuple-element.379, s32[]{:T(128)} %get-tuple-element.363), kind=kOutput, calls=%fused_computation.6.clone.1 | convolution fusion | flops 1611661312 | bytes 8913412 | tf_op jit(solution)/shard_map/while/body/eval_jaxpr/sab,subc->suac/dot_general | solution.py:27
  174.4 7.2 %collective-permute-start.7 = (f32[4,16,128,128]{3,2,1,0:T(8,128)}, f32[4,16,128,128]{3,2,1,0:T(8,128)}, u32[]{:S(2)}, u32[]{:S(2)}) collective-permute-start(f32[4,16,128,128]{3,2,1,0:T(8,128)} %copy.10), channel_id=1, source_target_pairs={{1,0},{2,1},{3,2},{4,3},{5,4},{6,5},{7,6},{8,7},{9,8},{10,9},{11,1... | collective-permute-start | bytes 12582920 | tf_op jit(solution)/shard_map/ppermute | solution.py:15
  181.6 7.2 %collective-permute-start.5 = (s32[4,16]{1,0:T(4,128)S(1)}, s32[4,16]{1,0:T(4,128)S(1)}, u32[]{:S(2)}, u32[]{:S(2)}) collective-permute-start(s32[4,16]{1,0:T(4,128)S(1)} %get-tuple-element.414), channel_id=1, source_target_pairs={{1,0},{2,1},{3,2},{4,3},{5,4},{6,5},{7,6},{8,7},{9,8},{10,9},{11,1... | collective-permute-start | bytes 776 | tf_op jit(solution)/shard_map/ppermute | solution.py:15
  188.8 84.0 %collective-permute-done.4 = s32[4,16]{1,0:T(4,128)S(1)} collective-permute-done((s32[4,16]{1,0:T(4,128)S(1)}, s32[4,16]{1,0:T(4,128)S(1)}, u32[]{:S(2)}, u32[]{:S(2)}) %collective-permute-start.4) | collective-permute-done | bytes 288 | tf_op jit(solution)/shard_map/ppermute | solution.py:15
  272.8 6.3 %fusion.48 = f32[4,24,128,128]{3,1,2,0:T(8,128)} fusion(f32[4,16,128,128]{3,1,2,0:T(8,128)} %get-tuple-element.208, s32[4,16]{1,0:T(4,128)S(1)} %get-tuple-element.414, s32[4,24]{1,0:T(4,128)S(1)} %copy-done.2, pred[4,24]{1,0:T(4,128)(4,1)S(1)} %get-tuple-element.247), kind=kOutput, calls=%fused_computation.83 | convolution fusion | flops 301992960 | bytes 10486496 | tf_op jit(solution)/shard_map/rts,rsab->rtab/dot_general | solution.py:52
  279.1 9.5 %pad_maximum_fusion = f32[12,16,128,128]{3,2,1,0:T(8,128)} fusion(f32[4,16,128,128]{3,2,1,0:T(8,128)} %collective-permute-done.7, f32[4,16,128,128]{3,2,1,0:T(8,128)} %copy.10, f32[4,16,128,128]{3,2,1,0:T(8,128)} %collective-permute-done.6), kind=kLoop, calls=%fused_computation.79 | loop fusion | flops 6291456 | bytes 25165824 | tf_op jit(solution)/shard_map/concatenate | solution.py:73
  288.6 169.4 %while.25 = (s32[]{:T(128)}, f32[4,24,128,128]{3,1,2,0:T(8,128)}, s32[4,8]{1,0:T(4,128)S(1)}, s32[]{:T(128)}, s32[12,16]{1,0:T(8,128)S(1)}, /*index=5*/s32[4,24]...) while((s32[]{:T(128)}, f32[4,24,128,128]{3,1,2,0:T(8,128)}, ...), condition=%wide.region_3.4_spmd, body=%wide.region_2.3_spmd.sunk | while | flops 3827310080 | bytes 60825748 | solution.py:45
  288.6 8.9 %gather_fusion.2 = f32[8,16,128,128]{3,2,1,0:T(8,128)} fusion(f32[12,16,128,128]{3,2,1,0:T(8,128)} %get-tuple-element.405, s32[1024]{0:T(1024)S(1)} %pad_clamp_fusion.5), kind=kCustom, calls=%fused_computation.3.clone.1 | custom fusion | bytes 16777248 | tf_op jit(solution)/shard_map/while/body/eval_jaxpr/jit(_take)/gather | solution.py:25
  297.6 16.9 %fusion.84 = f32[8,16,128,128]{3,2,1,0:T(8,128)} fusion(f32[8,16,128,128]{3,2,1,0:T(8,128)} %gather_fusion.2, pred[8]{0:T(512)(128)(4,1)S(1)} %compare_and_fusion.5, f32[4,8,128,128]{3,2,1,0:T(8,128)S(1)} %get-tuple-element.406, s32[]{:T(128)} %get-tuple-element.390), kind=kOutput, calls=%fused_computation.44.clone.1 | convolution fusion | flops 3223322624 | bytes 17302020 | tf_op jit(solution)/shard_map/while/body/eval_jaxpr/sab,subc->suac/dot_general | solution.py:27
  314.5 9.2 %copy.24 = f32[8,16,128,128]{2,1,0,3:T(8,128)} copy(f32[8,16,128,128]{3,2,1,0:T(8,128)} %fusion.84) | data formatting | bytes 16777216 | tf_op jit(solution)/shard_map/while/body/eval_jaxpr/sab,subc->suac/dot_general | solution.py:27
  324.3 6.6 %bitcast_dynamic-update-slice_fusion.2 = f32[4,24,128,128]{3,1,2,0:T(8,128)} fusion(f32[4,24,128,128]{3,1,2,0:T(8,128)} %get-tuple-element.391, s32[]{:T(128)} %get-tuple-element.390, f32[8,16,128,128]{2,1,0,3:T(8,128)} %copy.24, s32[24]{0:T(128)S(1)} %get-tuple-element.352, s32[8,16]{1,0:T(8,128)S(1)} %broadcast_select_fusion.6, ...), kind=kOutput, calls=%fused_computation.48.clone.1 | convolution fusion | flops 603985920 | bytes 9962616 | tf_op jit(solution)/shard_map/while/body/eval_jaxpr/fpn,pngi->fgi/dot_general | solution.py:37
  331.0 8.9 %gather_fusion.2 = f32[8,16,128,128]{3,2,1,0:T(8,128)} fusion(f32[12,16,128,128]{3,2,1,0:T(8,128)} %get-tuple-element.405, s32[1024]{0:T(1024)S(1)} %pad_clamp_fusion.5), kind=kCustom, calls=%fused_computation.3.clone.1 | custom fusion | bytes 16777248 | tf_op jit(solution)/shard_map/while/body/eval_jaxpr/jit(_take)/gather | solution.py:25
  339.9 16.9 %fusion.84 = f32[8,16,128,128]{3,2,1,0:T(8,128)} fusion(f32[8,16,128,128]{3,2,1,0:T(8,128)} %gather_fusion.2, pred[8]{0:T(512)(128)(4,1)S(1)} %compare_and_fusion.5, f32[4,8,128,128]{3,2,1,0:T(8,128)S(1)} %get-tuple-element.406, s32[]{:T(128)} %get-tuple-element.390), kind=kOutput, calls=%fused_computation.44.clone.1 | convolution fusion | flops 3223322624 | bytes 17302020 | tf_op jit(solution)/shard_map/while/body/eval_jaxpr/sab,subc->suac/dot_general | solution.py:27
  356.8 9.2 %copy.24 = f32[8,16,128,128]{2,1,0,3:T(8,128)} copy(f32[8,16,128,128]{3,2,1,0:T(8,128)} %fusion.84) | data formatting | bytes 16777216 | tf_op jit(solution)/shard_map/while/body/eval_jaxpr/sab,subc->suac/dot_general | solution.py:27
  366.7 6.6 %bitcast_dynamic-update-slice_fusion.2 = f32[4,24,128,128]{3,1,2,0:T(8,128)} fusion(f32[4,24,128,128]{3,1,2,0:T(8,128)} %get-tuple-element.391, s32[]{:T(128)} %get-tuple-element.390, f32[8,16,128,128]{2,1,0,3:T(8,128)} %copy.24, s32[24]{0:T(128)S(1)} %get-tuple-element.352, s32[8,16]{1,0:T(8,128)S(1)} %broadcast_select_fusion.6, ...), kind=kOutput, calls=%fused_computation.48.clone.1 | convolution fusion | flops 603985920 | bytes 9962616 | tf_op jit(solution)/shard_map/while/body/eval_jaxpr/fpn,pngi->fgi/dot_general | solution.py:37
  373.3 8.9 %gather_fusion.2 = f32[8,16,128,128]{3,2,1,0:T(8,128)} fusion(f32[12,16,128,128]{3,2,1,0:T(8,128)} %get-tuple-element.405, s32[1024]{0:T(1024)S(1)} %pad_clamp_fusion.5), kind=kCustom, calls=%fused_computation.3.clone.1 | custom fusion | bytes 16777248 | tf_op jit(solution)/shard_map/while/body/eval_jaxpr/jit(_take)/gather | solution.py:25
  382.3 16.9 %fusion.84 = f32[8,16,128,128]{3,2,1,0:T(8,128)} fusion(f32[8,16,128,128]{3,2,1,0:T(8,128)} %gather_fusion.2, pred[8]{0:T(512)(128)(4,1)S(1)} %compare_and_fusion.5, f32[4,8,128,128]{3,2,1,0:T(8,128)S(1)} %get-tuple-element.406, s32[]{:T(128)} %get-tuple-element.390), kind=kOutput, calls=%fused_computation.44.clone.1 | convolution fusion | flops 3223322624 | bytes 17302020 | tf_op jit(solution)/shard_map/while/body/eval_jaxpr/sab,subc->suac/dot_general | solution.py:27
  399.2 9.2 %copy.24 = f32[8,16,128,128]{2,1,0,3:T(8,128)} copy(f32[8,16,128,128]{3,2,1,0:T(8,128)} %fusion.84) | data formatting | bytes 16777216 | tf_op jit(solution)/shard_map/while/body/eval_jaxpr/sab,subc->suac/dot_general | solution.py:27
  409.0 6.6 %bitcast_dynamic-update-slice_fusion.2 = f32[4,24,128,128]{3,1,2,0:T(8,128)} fusion(f32[4,24,128,128]{3,1,2,0:T(8,128)} %get-tuple-element.391, s32[]{:T(128)} %get-tuple-element.390, f32[8,16,128,128]{2,1,0,3:T(8,128)} %copy.24, s32[24]{0:T(128)S(1)} %get-tuple-element.352, s32[8,16]{1,0:T(8,128)S(1)} %broadcast_select_fusion.6, ...), kind=kOutput, calls=%fused_computation.48.clone.1 | convolution fusion | flops 603985920 | bytes 9962616 | tf_op jit(solution)/shard_map/while/body/eval_jaxpr/fpn,pngi->fgi/dot_general | solution.py:37
  415.6 8.9 %gather_fusion.2 = f32[8,16,128,128]{3,2,1,0:T(8,128)} fusion(f32[12,16,128,128]{3,2,1,0:T(8,128)} %get-tuple-element.405, s32[1024]{0:T(1024)S(1)} %pad_clamp_fusion.5), kind=kCustom, calls=%fused_computation.3.clone.1 | custom fusion | bytes 16777248 | tf_op jit(solution)/shard_map/while/body/eval_jaxpr/jit(_take)/gather | solution.py:25
  424.6 16.9 %fusion.84 = f32[8,16,128,128]{3,2,1,0:T(8,128)} fusion(f32[8,16,128,128]{3,2,1,0:T(8,128)} %gather_fusion.2, pred[8]{0:T(512)(128)(4,1)S(1)} %compare_and_fusion.5, f32[4,8,128,128]{3,2,1,0:T(8,128)S(1)} %get-tuple-element.406, s32[]{:T(128)} %get-tuple-element.390), kind=kOutput, calls=%fused_computation.44.clone.1 | convolution fusion | flops 3223322624 | bytes 17302020 | tf_op jit(solution)/shard_map/while/body/eval_jaxpr/sab,subc->suac/dot_general | solution.py:27
  441.5 9.2 %copy.24 = f32[8,16,128,128]{2,1,0,3:T(8,128)} copy(f32[8,16,128,128]{3,2,1,0:T(8,128)} %fusion.84) | data formatting | bytes 16777216 | tf_op jit(solution)/shard_map/while/body/eval_jaxpr/sab,subc->suac/dot_general | solution.py:27
  451.3 6.6 %bitcast_dynamic-update-slice_fusion.2 = f32[4,24,128,128]{3,1,2,0:T(8,128)} fusion(f32[4,24,128,128]{3,1,2,0:T(8,128)} %get-tuple-element.391, s32[]{:T(128)} %get-tuple-element.390, f32[8,16,128,128]{2,1,0,3:T(8,128)} %copy.24, s32[24]{0:T(128)S(1)} %get-tuple-element.352, s32[8,16]{1,0:T(8,128)S(1)} %broadcast_select_fusion.6, ...), kind=kOutput, calls=%fused_computation.48.clone.1 | convolution fusion | flops 603985920 | bytes 9962616 | tf_op jit(solution)/shard_map/while/body/eval_jaxpr/fpn,pngi->fgi/dot_general | solution.py:37
  (89 shorter events, 80.9 us)
Async XLA Ops:
  3.1 54.6 %collective-permute-start.2 = (f32[4,8,128,128]{3,2,1,0:T(8,128)S(1)}, f32[4,8,128,128]{3,2,1,0:T(8,128)}, u32[]{:S(2)}, u32[]{:S(2)}) collective-permute-start(f32[4,8,128,128]{3,2,1,0:T(8,128)S(1)} %broadcast_select_fusion.2), channel_id=1, source_target_pairs={{255,0},{0,1},{1,2},{2,3},{3,4},{4,5},{5,6},{6,7},{7,8},{8,9},{9,1... | collective-permute-start | bytes 6291464 | tf_op jit(solution)/shard_map/ppermute | solution.py:15
  3.2 54.5 %collective-permute-start.3 = (f32[4,8,128,128]{3,2,1,0:T(8,128)S(1)}, f32[4,8,128,128]{3,2,1,0:T(8,128)}, u32[]{:S(2)}, u32[]{:S(2)}) collective-permute-start(f32[4,8,128,128]{3,2,1,0:T(8,128)S(1)} %broadcast_select_fusion.2), channel_id=1, source_target_pairs={{1,0},{2,1},{3,2},{4,3},{5,4},{6,5},{7,6},{8,7},{9,8},{10,9},{11,1... | collective-permute-start | bytes 6291464 | tf_op jit(solution)/shard_map/ppermute | solution.py:15
  11.5 45.5 %collective-permute-start = (s32[4,8]{1,0:T(4,128)}, s32[4,8]{1,0:T(4,128)S(1)}, u32[]{:S(2)}, u32[]{:S(2)}) collective-permute-start(s32[4,8]{1,0:T(4,128)} %param.9), channel_id=1, source_target_pairs={{255,0},{0,1},{1,2},{2,3},{3,4},{4,5},{5,6},{6,7},{7,8},{8,9},{9,1... | collective-permute-start | bytes 392 | tf_op jit(solution)/shard_map/ppermute | solution.py:15
  11.5 45.5 %collective-permute-start.1 = (s32[4,8]{1,0:T(4,128)}, s32[4,8]{1,0:T(4,128)S(1)}, u32[]{:S(2)}, u32[]{:S(2)}) collective-permute-start(s32[4,8]{1,0:T(4,128)} %param.9), channel_id=1, source_target_pairs={{1,0},{2,1},{3,2},{4,3},{5,4},{6,5},{7,6},{8,7},{9,8},{10,9},{11,1... | collective-permute-start | bytes 392 | tf_op jit(solution)/shard_map/ppermute | solution.py:15
  57.7 5.6 %copy-start = (s32[4,8]{1,0:T(4,128)S(1)}, s32[4,8]{1,0:T(4,128)}, u32[]{:S(2)}) copy-start(s32[4,8]{1,0:T(4,128)} %param.9) | copy-start | bytes 388
  57.7 5.6 %copy-start.1 = (s32[4,16]{1,0:T(4,128)S(1)}, s32[4,16]{1,0:T(4,128)}, u32[]{:S(2)}) copy-start(s32[4,16]{1,0:T(4,128)} %param.10) | copy-start | bytes 772
  168.9 19.9 %copy-start.2 = (s32[4,24]{1,0:T(4,128)S(1)}, s32[4,24]{1,0:T(4,128)}, u32[]{:S(2)}) copy-start(s32[4,24]{1,0:T(4,128)} %param.11) | copy-start | bytes 1156
  174.4 104.7 %collective-permute-start.6 = (f32[4,16,128,128]{3,2,1,0:T(8,128)}, f32[4,16,128,128]{3,2,1,0:T(8,128)}, u32[]{:S(2)}, u32[]{:S(2)}) collective-permute-start(f32[4,16,128,128]{3,2,1,0:T(8,128)} %copy.10), channel_id=1, source_target_pairs={{255,0},{0,1},{1,2},{2,3},{3,4},{4,5},{5,6},{6,7},{7,8},{8,9},{9,1... | collective-permute-start | bytes 12582920 | tf_op jit(solution)/shard_map/ppermute | solution.py:15
  174.4 104.7 %collective-permute-start.7 = (f32[4,16,128,128]{3,2,1,0:T(8,128)}, f32[4,16,128,128]{3,2,1,0:T(8,128)}, u32[]{:S(2)}, u32[]{:S(2)}) collective-permute-start(f32[4,16,128,128]{3,2,1,0:T(8,128)} %copy.10), channel_id=1, source_target_pairs={{1,0},{2,1},{3,2},{4,3},{5,4},{6,5},{7,6},{8,7},{9,8},{10,9},{11,1... | collective-permute-start | bytes 12582920 | tf_op jit(solution)/shard_map/ppermute | solution.py:15
  181.6 91.2 %collective-permute-start.4 = (s32[4,16]{1,0:T(4,128)S(1)}, s32[4,16]{1,0:T(4,128)S(1)}, u32[]{:S(2)}, u32[]{:S(2)}) collective-permute-start(s32[4,16]{1,0:T(4,128)S(1)} %get-tuple-element.414), channel_id=1, source_target_pairs={{255,0},{0,1},{1,2},{2,3},{3,4},{4,5},{5,6},{6,7},{7,8},{8,9},{9,1... | collective-permute-start | bytes 776 | tf_op jit(solution)/shard_map/ppermute | solution.py:15
  181.6 91.2 %collective-permute-start.5 = (s32[4,16]{1,0:T(4,128)S(1)}, s32[4,16]{1,0:T(4,128)S(1)}, u32[]{:S(2)}, u32[]{:S(2)}) collective-permute-start(s32[4,16]{1,0:T(4,128)S(1)} %get-tuple-element.414), channel_id=1, source_target_pairs={{1,0},{2,1},{3,2},{4,3},{5,4},{6,5},{7,6},{8,7},{9,8},{10,9},{11,1... | collective-permute-start | bytes 776 | tf_op jit(solution)/shard_map/ppermute | solution.py:15
where the time goes:
time: 469 us; the launch traced here: 467 us
  matrix products  159 us (34%)
  local copies, waits for them, and re-layouts  130 us (28%)
  waiting for transfers between devices  122 us (26%)
  starting transfers between devices  29.9 us (6%)
  other arithmetic  24.7 us (5%)
    ppermute x8, waiting for transfers between devices, passed_along(): return lax.ppermute(block, axis, route)  122 us
    dot_general x8, matrix products, one_row(): jnp.einsum('sab,subc->suac', blocks, selected_entries, precision=EXACT_AR...  108 us
    gather x8, local copies, waits for them, and re-layouts, one_row(): selected_entries = jnp.take(right_blocks, slot_rows, axis=0)  58.2 us
    dot_general x8, local copies, waits for them, and re-layouts, one_row(): jnp.einsum('sab,subc->suac', blocks, selected_entries, precision=EXACT_AR...  58.1 us
    dot_general x8, matrix products, one_row(): jnp.einsum('fpn,pngi->fgi', matching_entries, block_products_list, precis...  45.3 us
    ppermute x8, starting transfers between devices, passed_along(): return lax.ppermute(block, axis, route)  29.9 us
    concatenate x4, other arithmetic, gather_rim(): joined.append(jnp.concatenate(stacked, axis=0))  15.8 us
  transfers between devices with their start and end apart: 8, of which 2 were waited for; matrix products, arithmetic and copies ran while one was open for 1% of the time, Pallas kernels for 0%

commit v1 on v0

v1 whole, which is shorter than its diff:
```python
import functools

import jax
import jax.numpy as jnp
from jax import lax
from jax.experimental import pallas as pl
from jax.experimental.pallas import tpu as pltpu
from jax.sharding import PartitionSpec as P

AXES = ("row", "col")
ROWS, KP, KS, KC, BS = 4, 8, 16, 24, 128
UNROLL = 4
GROUP = 2 * UNROLL
CAP = (192 * KP + GROUP, 96 * KP + GROUP, 128 * KP + GROUP, 96 * KP + GROUP)
OFF = (0, CAP[0], CAP[0] + CAP[1], CAP[0] + CAP[1] + CAP[2])
TOTAL = sum(CAP)
ZERO_P = 96
VMEM_LIMIT = 60 * 1024 * 1024


def shifted(x, distance):
    n = lax.axis_size(AXES)
    return lax.ppermute(x, AXES, [((i - distance) % n, i) for i in range(n)])


def list_kernel(total_rows, base_ref, pat_ref, sq_ref, cu_ref, lists_ref, counts_ref, carry_ref, pos_p, pos_s):
    wrap = total_rows - 1
    base = base_ref[0]

    def clear(ref, size):
        def step(i, _):
            for q in range(8):
                ref[i * 8 + q] = -1
            return 0

        lax.fori_loop(0, size // 8, step, 0)

    clear(pos_p, 20 * 16)
    clear(pos_s, 12 * 32)

    def place_p(r, _):
        for u in range(KP):
            col = pat_ref[r * KP + u]

            @pl.when(col >= 0)
            def _():
                pos_p[r * 16 + jnp.minimum((col - base - r + 4) & wrap, 15)] = u

        return 0

    lax.fori_loop(0, 20, place_p, 0)

    def place_s(r, _):
        for u in range(KS):
            col = sq_ref[r * KS + u]

            @pl.when(col >= 0)
            def _():
                pos_s[r * 32 + jnp.minimum((col - base - 4 - r + 8) & wrap, 31)] = u

        return 0

    lax.fori_loop(0, 12, place_s, 0)

    def filler(zero_right):
        return ZERO_P | (zero_right << 8)

    def even(p, off, zero_right):
        lists_ref[off + p] = filler(zero_right)
        return p + (p & 1)

    def square_target(idx, carry):
        k = idx // KS
        col = sq_ref[idx]
        pa, pb = carry
        live = col >= 0
        for s in range(KP):
            m = pat_ref[(k + 4) * KP + s]
            mloc = jnp.minimum((m - base) & wrap, 19)
            u = pos_p[mloc * 16 + jnp.minimum((col - m + 4) & wrap, 15)]
            hit = jnp.logical_and(jnp.logical_and(live, m >= 0), u >= 0)
            near = jnp.logical_and(mloc >= 4, mloc < 16)
            left = (k * KP + s) | (idx << 16)
            lists_ref[OFF[0] + pa] = left | (((mloc - 4) * KP + u) << 8)
            far = jnp.where(mloc < 4, mloc, mloc - 12)
            lists_ref[OFF[2] + pb] = left | ((far * KP + u) << 8)
            pa = pa + jnp.where(jnp.logical_and(hit, near), 1, 0)
            pb = pb + jnp.where(jnp.logical_and(hit, jnp.logical_not(near)), 1, 0)
        return even(pa, OFF[0], 96), even(pb, OFF[2], 64)

    na, nc = lax.fori_loop(0, 12 * KS, square_target, (jnp.int32(0), jnp.int32(0)))

    def cube_target(idx, carry):
        i = idx // KC
        col = cu_ref[idx]
        pa, pb = carry
        live = col >= 0
        for s in range(KP):
            k = pat_ref[(i + 8) * KP + s]
            kloc = jnp.minimum((k - base - 4) & wrap, 11)
            u = pos_s[kloc * 32 + jnp.minimum((col - k + 8) & wrap, 31)]
            hit = jnp.logical_and(jnp.logical_and(live, k >= 0), u >= 0)
            near = jnp.logical_and(kloc >= 4, kloc < 8)
            left = ((i + 4) * KP + s) | (idx << 16)
            lists_ref[OFF[1] + pa] = left | (((kloc - 4) * KS + u) << 8)
            far = jnp.where(kloc < 4, kloc, kloc - 4)
            lists_ref[OFF[3] + pb] = left | ((far * KS + u) << 8)
            pa = pa + jnp.where(jnp.logical_and(hit, near), 1, 0)
            pb = pb + jnp.where(jnp.logical_and(hit, jnp.logical_not(near)), 1, 0)
        u = pos_s[(i + 4) * 32 + jnp.minimum((col - base - 8 - i + 8) & wrap, 31)]
        carry_ref[idx] = jnp.where(jnp.logical_and(live, u >= 0), i * KS + u, 64)
        return even(pa, OFF[1], 64), even(pb, OFF[3], 128)

    nb, nd = lax.fori_loop(0, 4 * KC, cube_target, (jnp.int32(0), jnp.int32(0)))

    for which, (n, zero_right) in enumerate(((na, 96), (nb, 64), (nc, 64), (nd, 128))):
        for q in range(GROUP):
            lists_ref[OFF[which] + n + q] = filler(zero_right)
        counts_ref[which] = (n + GROUP - 1) // GROUP


def pair_lists(base, pat20, sq12, cu4, total_rows):
    smem = pl.BlockSpec(memory_space=pltpu.SMEM)
    return pl.pallas_call(
        functools.partial(list_kernel, total_rows),
        out_shape=(
            jax.ShapeDtypeStruct((TOTAL,), jnp.int32),
            jax.ShapeDtypeStruct((4,), jnp.int32),
            jax.ShapeDtypeStruct((4 * KC,), jnp.int32),
        ),
        in_specs=[smem] * 4,
        out_specs=(smem,) * 3,
        scratch_shapes=[pltpu.SMEM((20 * 16,), jnp.int32), pltpu.SMEM((12 * 32,), jnp.int32)],
        cost_estimate=pl.CostEstimate(flops=20_000_000, bytes_accessed=40_000_000, transcendentals=0),
        name="pair_lists",
    )(base, pat20, sq12, cu4)


def halves(x):
    hi = x.astype(jnp.bfloat16)
    lo = (x - hi.astype(jnp.float32)).astype(jnp.bfloat16)
    return hi, lo


def put_left(ref, at, hi, lo):
    ref[at, 0:BS, :] = hi
    ref[at, BS : 2 * BS, :] = lo


def put_right(ref, at, hi, lo):
    ref[at, :, 0:BS] = hi
    ref[at, :, BS : 2 * BS] = lo


def multiply(lists_ref, off, groups, left, right, total):
    def group(g, _):
        at = off + g * GROUP
        done = []
        for x in range(UNROLL):
            e, f = lists_ref[at + 2 * x], lists_ref[at + 2 * x + 1]
            lhs = jnp.concatenate([left[e & 255], left[f & 255]], axis=1)
            rhs = jnp.concatenate([right[(e >> 8) & 255], right[(f >> 8) & 255]], axis=0)
            r = jnp.dot(lhs, rhs, preferred_element_type=jnp.float32)
            done.append((e >> 16, (r[:BS, :BS] + r[:BS, BS:]) + (r[BS:, :BS] + r[BS:, BS:])))
        for t, q in done:
            total[t] = total[t] + q
        return 0

    lax.fori_loop(0, groups, group, 0)


def near_kernel(lists, counts, below, own, above, s_out, sp_out, c_out, left_out, right, total, s_right):
    zero_l = jnp.zeros((2 * BS, BS), jnp.bfloat16)
    zero_r = jnp.zeros((BS, 2 * BS), jnp.bfloat16)
    left_out[ZERO_P] = zero_l
    right[96] = zero_r
    s_right[64] = zero_r
    for part, src in enumerate((below, own, above)):

        def cut(q, _):
            hi, lo = halves(src[q // KP, q % KP])
            put_left(left_out, part * 32 + q, hi, lo)
            put_right(right, part * 32 + q, hi, lo)
            return 0

        lax.fori_loop(0, 32, cut, 0)

    def clear(ref, n):
        def step(q, _):
            ref[q] = jnp.zeros((BS, BS), jnp.float32)
            return 0

        lax.fori_loop(0, n, step, 0)

    clear(total, 192)
    clear(c_out, 96)
    multiply(lists, OFF[0], counts[0], left_out, right, total)

    def share(q, _):
        x = total[64 + q]
        s_out[q] = x
        hi, lo = halves(x)
        put_right(s_right, q, hi, lo)
        sp_out[q] = total[q]
        sp_out[64 + q] = total[128 + q]
        return 0

    lax.fori_loop(0, 64, share, 0)
    multiply(lists, OFF[1], counts[1], left_out, s_right, c_out)


def near_step(lists, counts, below, own, above):
    smem = pl.BlockSpec(memory_space=pltpu.SMEM)
    vmem = pl.BlockSpec(memory_space=pltpu.VMEM)
    return pl.pallas_call(
        near_kernel,
        out_shape=(
            jax.ShapeDtypeStruct((64, BS, BS), jnp.float32),
            jax.ShapeDtypeStruct((128, BS, BS), jnp.float32),
            jax.ShapeDtypeStruct((96, BS, BS), jnp.float32),
            jax.ShapeDtypeStruct((97, 2 * BS, BS), jnp.bfloat16),
        ),
        in_specs=[smem, smem, vmem, vmem, vmem],
        out_specs=(vmem,) * 4,
        scratch_shapes=[
            pltpu.VMEM((97, BS, 2 * BS), jnp.bfloat16),
            pltpu.VMEM((192, BS, BS), jnp.float32),
            pltpu.VMEM((65, BS, 2 * BS), jnp.bfloat16),
        ],
        compiler_params=pltpu.CompilerParams(vmem_limit_bytes=VMEM_LIMIT),
        cost_estimate=pl.CostEstimate(flops=8_000_000_000, bytes_accessed=60_000_000, transcendentals=0),
        name="near_step",
    )(lists, counts, below, own, above)


def far_kernel(lists, counts, carry, below, above, left, sp, c_in, s_own, out, right, s_right):
    zero_r = jnp.zeros((BS, 2 * BS), jnp.bfloat16)
    right[64] = zero_r
    s_right[128] = zero_r
    for part, src in enumerate((below, above)):

        def cut(q, _):
            hi, lo = halves(src[q // KP, q % KP])
            put_right(right, part * 32 + q, hi, lo)
            return 0

        lax.fori_loop(0, 32, cut, 0)

    def far_total(t):
        return jnp.where(t >= 128, t - 64, t)

    def group(g, _):
        at = OFF[2] + g * GROUP
        done = []
        for x in range(UNROLL):
            e, f = lists[at + 2 * x], lists[at + 2 * x + 1]
            lhs = jnp.concatenate([left[e & 255], left[f & 255]], axis=1)
            rhs = jnp.concatenate([right[(e >> 8) & 255], right[(f >> 8) & 255]], axis=0)
            r = jnp.dot(lhs, rhs, preferred_element_type=jnp.float32)
            done.append((far_total(e >> 16), (r[:BS, :BS] + r[:BS, BS:]) + (r[BS:, :BS] + r[BS:, BS:])))
        for t, q in done:
            sp[t] = sp[t] + q
        return 0

    lax.fori_loop(0, counts[2], group, 0)

    def share(q, _):
        hi, lo = halves(sp[q])
        put_right(s_right, q, hi, lo)
        return 0

    lax.fori_loop(0, 128, share, 0)
    multiply(lists, OFF[3], counts[3], left, s_right, c_in)

    def finish(q, _):
        at = carry[q]
        kept = jnp.where(at < 64, 3.0, 0.0)
        out[q] = kept * s_own[jnp.minimum(at, 63)] - 2.0 * c_in[q]
        return 0

    lax.fori_loop(0, 96, finish, 0)


def far_step(lists, counts, carry, below, above, left, sp, c_in, s_own):
    smem = pl.BlockSpec(memory_space=pltpu.SMEM)
    vmem = pl.BlockSpec(memory_space=pltpu.VMEM)
    return pl.pallas_call(
        far_kernel,
        out_shape=jax.ShapeDtypeStruct((96, BS, BS), jnp.float32),
        in_specs=[smem] * 3 + [vmem] * 6,
        out_specs=vmem,
        scratch_shapes=[
            pltpu.VMEM((65, BS, 2 * BS), jnp.bfloat16),
            pltpu.VMEM((129, BS, 2 * BS), jnp.bfloat16),
        ],
        compiler_params=pltpu.CompilerParams(vmem_limit_bytes=VMEM_LIMIT),
        cost_estimate=pl.CostEstimate(flops=8_000_000_000, bytes_accessed=60_000_000, transcendentals=0),
        name="far_step",
    )(lists, counts, carry, below, above, left, sp, c_in, s_own)


def local(density, pattern, square_target, cube_target):
    total_rows = ROWS * lax.axis_size(AXES)
    first_row = lax.axis_index(AXES) * ROWS
    base = jnp.remainder(first_row - 2 * ROWS, total_rows).astype(jnp.int32).reshape(1)

    cols = jnp.concatenate([pattern, square_target], axis=1)
    m1, p1, m2, p2 = (shifted(cols, d) for d in (1, -1, 2, -2))
    density, m1, p1, m2, p2 = lax.optimization_barrier((density, m1, p1, m2, p2))
    below = shifted(density, 1)
    above = shifted(density, -1)
    pat20 = jnp.concatenate([m2[:, :KP], m1[:, :KP], pattern, p1[:, :KP], p2[:, :KP]], axis=0).reshape(-1)
    sq12 = jnp.concatenate([m1[:, KP:], square_target, p1[:, KP:]], axis=0).reshape(-1)
    lists, counts, carry = pair_lists(base, pat20, sq12, cube_target.reshape(-1), total_rows)
    below, above, lists, counts, carry = lax.optimization_barrier((below, above, lists, counts, carry))
    below2 = shifted(below, 1)
    above2 = shifted(above, -1)
    s_own, sp, c_part, left = near_step(lists, counts, below, density, above)
    out = far_step(lists, counts, carry, below2, above2, left, sp, c_part, s_own)
    return s_own.reshape(ROWS, KS, BS, BS), out.reshape(ROWS, KC, BS, BS)


def solution(mesh):
    in_specs = (P(AXES, None, None, None), P(AXES, None), P(AXES, None), P(AXES, None))
    out_specs = (P(AXES, None, None, None), P(AXES, None, None, None))
    return jax.shard_map(local, mesh=mesh, in_specs=in_specs, out_specs=out_specs, check_vma=False)
```

time: 469 us -> 151 us (0.32)
  matrix products: 159 us -> 0 us
  local copies, waits for them, and re-layouts: 130 us -> 4.8 us
  waiting for transfers between devices: 122 us -> 19 us
  Pallas kernels: 0 us -> 97.9 us
  other arithmetic: 24.7 us -> 1.46 us
  starting transfers between devices: 29.9 us -> 24.9 us
    dot_general x17 -> x0, matrix products: 159 us -> none  [the longest x8 108 us: one_row(): jnp.einsum('sab,subc->suac', blocks, selected_entries, precision=EXACT_AR...]
    ppermute x8, waiting for transfers between devices: 122 us -> 19 us  [shifted(): return lax.ppermute(x, AXES, [((i - distance) % n, i) for i in range(n)])]
    pallas_call x0 -> x3, Pallas kernels: none -> 97.9 us  [the longest x1 41 us: pair_lists(): pl.pallas_call(functools.partial(list_kernel, total_rows), out_shape=(jax...]
    gather x16 -> x0, local copies, waits for them, and re-layouts: 62.6 us -> none  [the longest x8 58.2 us: one_row(): selected_entries = jnp.take(right_blocks, slot_rows, axis=0)]
    dot_general x8 -> x0, local copies, waits for them, and re-layouts: 58.1 us -> none  [one_row(): jnp.einsum('sab,subc->suac', blocks, selected_entries, precision=EXACT_AR...]
    concatenate x4 -> x2, other arithmetic: 15.8 us -> 1.46 us  [the longest x1 0.77 us: local(): cols = jnp.concatenate([pattern, square_target], axis=1)]
    unnamed x8 -> x4, local copies, waits for them, and re-layouts: 9.33 us -> 1.34 us
    mul x1 -> x0, other arithmetic: 5.45 us -> none  [combine(): return kept_slots * (3.0 * carried - 2.0 * cubed)]
  transfers between devices with their start and end apart: 8 -> 8, of which waited for: 2 -> 4; matrix products, arithmetic and copies ran while one was open for 1% -> 3% of each run, Pallas kernels for 0% -> 50%
where the time goes in v1:
time: 151 us; the launch traced here: 149 us
  Pallas kernels  97.9 us (65%)
  starting transfers between devices  24.9 us (16%)
  waiting for transfers between devices  19 us (13%)
  local copies, waits for them, and re-layouts  4.8 us (3%)
    pallas_call x1, Pallas kernels, pair_lists(): pl.pallas_call(functools.partial(list_kernel, total_rows), out_shape=(jax...  41 us
    pallas_call x1, Pallas kernels, near_step(): pl.pallas_call(near_kernel, out_shape=(jax.ShapeDtypeStruct((64, BS, BS),...  33.1 us
    ppermute x8, starting transfers between devices, shifted(): return lax.ppermute(x, AXES, [((i - distance) % n, i) for i in range(n)])  24.9 us
    pallas_call x1, Pallas kernels, far_step(): pl.pallas_call(far_kernel, out_shape=jax.ShapeDtypeStruct((96, BS, BS), j...  23.8 us
    ppermute x8, waiting for transfers between devices, shifted(): return lax.ppermute(x, AXES, [((i - distance) % n, i) for i in range(n)])  19 us
  transfers between devices with their start and end apart: 8, of which 4 were waited for; matrix products, arithmetic and copies ran while one was open for 3% of the time, Pallas kernels for 50%

profile of v1, /device:TPU:0, one launch (start us, length us, event | category | flops | bytes accessed | tf_op | source)
XLA Modules:
  0.0 148.7 jit_solution(9580043904145579753)
XLA Ops:
  0.6 0.8 pad_add_fusion.1
  1.4 8.4 %collective-permute-start.3 = (s32[4,24]{1,0:T(4,128)S(1)}, s32[4,24]{1,0:T(4,128)S(1)}, u32[]{:S(2)}, u32[]{:S(2)}) collective-permute-start(s32[4,24]{1,0:T(4,128)S(1)} %pad_add_fusion.1), channel_id=1, source_target_pairs={{2,0},{3,1},{4,2},{5,3},{6,4},{7,5},{8,6},{9,7},{10,8},{11,9},{12,... | collective-permute-start | bytes 1160 | tf_op jit(solution)/shard_map/ppermute | solution.py:23
  9.8 0.0 collective-permute-start.2
  9.8 7.3 %collective-permute-start.1 = (s32[4,24]{1,0:T(4,128)S(1)}, s32[4,24]{1,0:T(4,128)S(1)}, u32[]{:S(2)}, u32[]{:S(2)}) collective-permute-start(s32[4,24]{1,0:T(4,128)S(1)} %pad_add_fusion.1), channel_id=1, source_target_pairs={{1,0},{2,1},{3,2},{4,3},{5,4},{6,5},{7,6},{8,7},{9,8},{10,9},{11,1... | collective-permute-start | bytes 1160 | tf_op jit(solution)/shard_map/ppermute | solution.py:23
  17.1 0.0 collective-permute-start
  17.1 0.0 collective-permute-done.3
  17.1 1.4 collective-permute-done.2
  18.5 0.0 collective-permute-done.1
  18.5 7.0 %collective-permute-done = s32[4,24]{1,0:T(4,128)S(1)} collective-permute-done((s32[4,24]{1,0:T(4,128)S(1)}, s32[4,24]{1,0:T(4,128)S(1)}, u32[]{:S(2)}, u32[]{:S(2)}) %collective-permute-start) | collective-permute-done | bytes 416 | tf_op jit(solution)/shard_map/ppermute | solution.py:23
  25.5 0.0 collective-permute-start.5
  25.5 2.0 %collective-permute-start.4 = (f32[4,8,128,128]{3,2,1,0:T(8,128)}, f32[4,8,128,128]{3,2,1,0:T(8,128)}, u32[]{:S(2)}, u32[]{:S(2)}) collective-permute-start(f32[4,8,128,128]{3,2,1,0:T(8,128)} %own), channel_id=1, source_target_pairs={{255,0},{0,1},{1,2},{2,3},{3,4},{4,5},{5,6},{6,7},{7,8},{8,9},{9,1... | collective-permute-start | bytes 6291464 | tf_op jit(solution)/shard_map/ppermute | solution.py:23
  27.5 1.3 reshape.25.cu_ref
  28.8 0.1 slice.22
  28.9 0.1 slice.23
  29.0 0.7 pad_add_fusion
  29.7 0.6 reshape.24.sq_ref
  30.3 0.7 concatenate.10
  31.0 0.7 reshape.23.pat_ref
  31.7 41.0 %pair_lists.1 = (s32[4128]{0:T(1024)}, s32[4]{0:T(128)}, s32[96]{0:T(128)}) custom-call(s32[1]{0:T(128)} %bitcast.base_ref, s32[160]{0:T(256)} %reshape.23.pat_ref, s32[192]{0:T(256)} %reshape.24.sq_ref, s32[96]{0:T(128)} %reshape.25.cu_ref), custom_call_target="tpu_custom_call" | custom-call | flops 20000000 | bytes 40000000 | tf_op jit(solution)/shard_map/pair_lists/pallas_call | solution.py:124
  72.7 0.0 collective-permute-done.5.above
  72.7 0.0 copy-start.1
  72.8 1.7 %collective-permute-done.4.below = f32[4,8,128,128]{3,2,1,0:T(8,128)} collective-permute-done((f32[4,8,128,128]{3,2,1,0:T(8,128)}, f32[4,8,128,128]{3,2,1,0:T(8,128)}, u32[]{:S(2)}, u32[]{:S(2)}) %collective-permute-start.4) | collective-permute-done | bytes 2097184 | tf_op jit(solution)/shard_map/ppermute | solution.py:23
  74.5 0.0 copy-done.1
  74.5 0.0 collective-permute-start.6
  74.5 7.2 %collective-permute-start.7 = (f32[4,8,128,128]{3,2,1,0:T(8,128)}, f32[4,8,128,128]{3,2,1,0:T(8,128)}, u32[]{:S(2)}, u32[]{:S(2)}) collective-permute-start(f32[4,8,128,128]{3,2,1,0:T(8,128)} %copy-done.1), channel_id=1, source_target_pairs={{1,0},{2,1},{3,2},{4,3},{5,4},{6,5},{7,6},{8,7},{9,8},{10,9},{11,1... | collective-permute-start | bytes 6291464 | tf_op jit(solution)/shard_map/ppermute | solution.py:23
  81.7 33.1 %near_step.1 = (f32[64,128,128]{2,1,0:T(8,128)}, f32[128,128,128]{2,1,0:T(8,128)}, f32[96,128,128]{2,1,0:T(8,128)}, bf16[97,256,128]{2,1,0:T(8,128)(2,1)}) custom-call(s32[4128]{0:T(1024)} %get-tuple-element.27.lists, s32[4]{0:T(128)} %get-tuple-element.28.counts, f32[4,8,128,128]{3,2,1,0:T(8,128)} %collective-permute-done.4.below, f32[4,8,128,128]{3,2,1,0:T(8,128)} %own, ...), custom_call_target="tpu_custom_call" | custom-call | flops 8000000000 | bytes 60000000 | tf_op jit(solution)/shard_map/near_step/pallas_call | solution.py:215
  114.7 8.8 %collective-permute-done.6.below = f32[4,8,128,128]{3,2,1,0:T(8,128)S(1)} collective-permute-done((f32[4,8,128,128]{3,2,1,0:T(8,128)}, f32[4,8,128,128]{3,2,1,0:T(8,128)S(1)}, u32[]{:S(2)}, u32[]{:S(2)}) %collective-permute-start.6) | collective-permute-done | bytes 2097184 | tf_op jit(solution)/shard_map/ppermute | solution.py:23
  123.6 0.0 copy-start
  123.6 0.0 collective-permute-done.7.above
  123.6 1.3 copy-done
  124.9 23.8 %far_step.1 = f32[96,128,128]{2,1,0:T(8,128)} custom-call(s32[4128]{0:T(1024)} %get-tuple-element.27.lists, s32[4]{0:T(128)} %get-tuple-element.28.counts, s32[96]{0:T(128)} %get-tuple-element.32.carry, f32[4,8,128,128]{3,2,1,0:T(8,128)} %copy-done, f32[4,8,128,128]{3,2,1,0:T(8,128)} %collective-permute-done.7.above, ...), custom_call_target="tpu_custom_call" | custom-call | flops 8000000000 | bytes 60000000 | tf_op jit(solution)/shard_map/far_step/pallas_call | solution.py:287
Async XLA Ops:
  1.4 15.7 %collective-permute-start.3 = (s32[4,24]{1,0:T(4,128)S(1)}, s32[4,24]{1,0:T(4,128)S(1)}, u32[]{:S(2)}, u32[]{:S(2)}) collective-permute-start(s32[4,24]{1,0:T(4,128)S(1)} %pad_add_fusion.1), channel_id=1, source_target_pairs={{2,0},{3,1},{4,2},{5,3},{6,4},{7,5},{8,6},{9,7},{10,8},{11,9},{12,... | collective-permute-start | bytes 1160 | tf_op jit(solution)/shard_map/ppermute | solution.py:23
  9.8 8.7 %collective-permute-start.2 = (s32[4,24]{1,0:T(4,128)S(1)}, s32[4,24]{1,0:T(4,128)S(1)}, u32[]{:S(2)}, u32[]{:S(2)}) collective-permute-start(s32[4,24]{1,0:T(4,128)S(1)} %pad_add_fusion.1), channel_id=1, source_target_pairs={{254,0},{255,1},{0,2},{1,3},{2,4},{3,5},{4,6},{5,7},{6,8},{7,9},{8... | collective-permute-start | bytes 1160 | tf_op jit(solution)/shard_map/ppermute | solution.py:23
  9.8 8.7 %collective-permute-start.1 = (s32[4,24]{1,0:T(4,128)S(1)}, s32[4,24]{1,0:T(4,128)S(1)}, u32[]{:S(2)}, u32[]{:S(2)}) collective-permute-start(s32[4,24]{1,0:T(4,128)S(1)} %pad_add_fusion.1), channel_id=1, source_target_pairs={{1,0},{2,1},{3,2},{4,3},{5,4},{6,5},{7,6},{8,7},{9,8},{10,9},{11,1... | collective-permute-start | bytes 1160 | tf_op jit(solution)/shard_map/ppermute | solution.py:23
  17.1 8.4 %collective-permute-start = (s32[4,24]{1,0:T(4,128)S(1)}, s32[4,24]{1,0:T(4,128)S(1)}, u32[]{:S(2)}, u32[]{:S(2)}) collective-permute-start(s32[4,24]{1,0:T(4,128)S(1)} %pad_add_fusion.1), channel_id=1, source_target_pairs={{255,0},{0,1},{1,2},{2,3},{3,4},{4,5},{5,6},{6,7},{7,8},{8,9},{9,1... | collective-permute-start | bytes 1160 | tf_op jit(solution)/shard_map/ppermute | solution.py:23
  25.5 47.2 %collective-permute-start.5 = (f32[4,8,128,128]{3,2,1,0:T(8,128)}, f32[4,8,128,128]{3,2,1,0:T(8,128)S(1)}, u32[]{:S(2)}, u32[]{:S(2)}) collective-permute-start(f32[4,8,128,128]{3,2,1,0:T(8,128)} %own), channel_id=1, source_target_pairs={{1,0},{2,1},{3,2},{4,3},{5,4},{6,5},{7,6},{8,7},{9,8},{10,9},{11,1... | collective-permute-start | bytes 6291464 | tf_op jit(solution)/shard_map/ppermute | solution.py:23
  25.5 49.0 %collective-permute-start.4 = (f32[4,8,128,128]{3,2,1,0:T(8,128)}, f32[4,8,128,128]{3,2,1,0:T(8,128)}, u32[]{:S(2)}, u32[]{:S(2)}) collective-permute-start(f32[4,8,128,128]{3,2,1,0:T(8,128)} %own), channel_id=1, source_target_pairs={{255,0},{0,1},{1,2},{2,3},{3,4},{4,5},{5,6},{6,7},{7,8},{8,9},{9,1... | collective-permute-start | bytes 6291464 | tf_op jit(solution)/shard_map/ppermute | solution.py:23
  72.7 1.8 %copy-start.1 = (f32[4,8,128,128]{3,2,1,0:T(8,128)}, f32[4,8,128,128]{3,2,1,0:T(8,128)S(1)}, u32[]{:S(2)}) copy-start(f32[4,8,128,128]{3,2,1,0:T(8,128)S(1)} %collective-permute-done.5.above) | copy-start | bytes 6291460
  74.5 49.1 %collective-permute-start.6 = (f32[4,8,128,128]{3,2,1,0:T(8,128)}, f32[4,8,128,128]{3,2,1,0:T(8,128)S(1)}, u32[]{:S(2)}, u32[]{:S(2)}) collective-permute-start(f32[4,8,128,128]{3,2,1,0:T(8,128)} %collective-permute-done.4.below), channel_id=1, source_target_pairs={{255,0},{0,1},{1,2},{2,3},{3,4},{4,5},{5,6},{6,7},{7,8},{8,9},{9,1... | collective-permute-start | bytes 6291464 | tf_op jit(solution)/shard_map/ppermute | solution.py:23
  74.5 49.1 %collective-permute-start.7 = (f32[4,8,128,128]{3,2,1,0:T(8,128)}, f32[4,8,128,128]{3,2,1,0:T(8,128)}, u32[]{:S(2)}, u32[]{:S(2)}) collective-permute-start(f32[4,8,128,128]{3,2,1,0:T(8,128)} %copy-done.1), channel_id=1, source_target_pairs={{1,0},{2,1},{3,2},{4,3},{5,4},{6,5},{7,6},{8,7},{9,8},{10,9},{11,1... | collective-permute-start | bytes 6291464 | tf_op jit(solution)/shard_map/ppermute | solution.py:23
  123.6 1.3 copy-start

commit v2 on v0

v2 whole, which is shorter than its diff:
```python
import functools

import jax
import jax.numpy as jnp
import numpy as np
from jax import lax
from jax.experimental import pallas as pl
from jax.experimental.pallas import tpu as pltpu
from jax.sharding import PartitionSpec as P

AXES = ("row", "col")
ROWS, KP, KS, KC, BS = 4, 8, 16, 24, 128
HALF = ROWS // 2
PIECE = HALF * KP
UNROLL = 8
GROUP = 2 * UNROLL
ZERO_LEFT = 12 * KP

OWN, MIDDLE, LAST = (4, 5, 6, 7), (2, 3, 8, 9), (0, 1, 10, 11)
ORDER = OWN + MIDDLE + LAST

TARGETS = (12 * KS, 4 * KC, 8 * KS, 4 * KC, 4 * KS, 4 * KC)
ZERO_RIGHT = (12 * KP, 4 * KS, 2 * PIECE, 4 * KS, 2 * PIECE, 4 * KS)
TABLE_OFF = tuple(int(x) for x in np.cumsum((0,) + tuple(t * KP for t in TARGETS)))
LIST_OFF = tuple(int(x) for x in np.cumsum((0,) + tuple(t * KP + GROUP for t in TARGETS)))


def shifted(x, distance):
    n = lax.axis_size(AXES)
    return lax.ppermute(x, AXES, [((i - distance) % n, i) for i in range(n)])


def lookup(rows, count):
    table = np.full((count,), -1, np.int32)
    table[list(rows)] = np.arange(len(rows))
    return table


def pair_tables(base, pat20, sq12, cu4, total_rows):
    def place(cols, start, count):
        return jnp.minimum(jnp.remainder(cols - start, total_rows), count - 1)

    def matched(left_cols, right_cols, targets):
        same = right_cols[:, None, :, :] == targets[:, :, None, None]
        same = same & (targets >= 0)[:, :, None, None] & (left_cols >= 0)[:, None, :, None]
        return jnp.max(jnp.where(same, jnp.arange(right_cols.shape[-1], dtype=jnp.int32), -1), axis=-1)

    def pick(table, index):
        hot = index[..., None] == jnp.arange(table.shape[0], dtype=jnp.int32)
        shape = hot.shape + (1,) * (table.ndim - 1)
        return jnp.sum(jnp.where(hot.reshape(shape), table, 0), axis=index.ndim)

    def entries(u, left, right_row, width, target):
        right = right_row[:, None, :] * width + u
        ok = (u >= 0) & (right_row >= 0)[:, None, :]
        return jnp.where(ok, left[:, None, :] | (right << 8) | (target[:, :, None] << 16), -1).reshape(-1, KP)

    def const(x):
        return jnp.asarray(np.asarray(x, np.int32))

    slots = np.arange(KP, dtype=np.int32)
    near_p = lookup(range(4, 16), 20)
    mid_p = lookup((2, 3, 16, 17), 20)
    last_p = lookup((0, 1, 18, 19), 20)

    pk = pat20[4:16]
    at = place(pk, base, 20)
    u = matched(pk, pick(pat20, at), sq12)
    left = const(np.arange(12)[:, None] * KP + slots)
    tables = {}
    for which, (rows, here) in enumerate(((ORDER, near_p), (MIDDLE + LAST, mid_p), (LAST, last_p))):
        sel = np.asarray(rows)
        target = const(np.arange(len(rows))[:, None] * KS + np.arange(KS))
        take = lambda x: jnp.stack([x[r] for r in rows])
        tables[2 * which] = entries(take(u), const(np.arange(12)[sel][:, None] * KP + slots), pick(const(here), take(at)), KP, target)

    pi = pat20[8:12]
    at = place(pi, base + 4, 12)
    u = matched(pi, pick(sq12, at), cu4)
    left = const((np.arange(4) + 4)[:, None] * KP + slots)
    target = const(np.arange(4)[:, None] * KC + np.arange(KC))
    for which, rows in enumerate((OWN, MIDDLE, LAST)):
        tables[2 * which + 1] = entries(u, left, pick(const(lookup(rows, 12)), at), KS, target)

    same = (cu4[:, :, None] == sq12[4:8][:, None, :]) & (cu4 >= 0)[:, :, None]
    slot = jnp.max(jnp.where(same, jnp.arange(KS, dtype=jnp.int32), -1), axis=-1)
    carry = jnp.where(slot >= 0, slot + const(np.arange(4)[:, None] * KS), -1).reshape(-1)
    table = jnp.concatenate([tables[i] for i in range(6)])
    hit = table >= 0
    rank = jnp.sum(jnp.where(hit[:, None, :] & (slots[None, :] < slots[:, None])[None], 1, 0), axis=-1)
    moved = hit[:, None, :] & (rank[:, None, :] == slots[None, :, None])
    filler = const(np.repeat([ZERO_LEFT | (z << 8) for z in ZERO_RIGHT], TARGETS))[:, None]
    packed = jnp.where(jnp.any(moved, axis=-1), jnp.sum(jnp.where(moved, table[:, None, :], 0), axis=-1), filler)
    return packed.reshape(-1), jnp.sum(hit.astype(jnp.int32), axis=-1), carry


def list_kernel(table, hits, lists, counts):
    start = 0
    for which in range(6):
        t0, l0 = TABLE_OFF[which], LIST_OFF[which]

        def target(i, n):
            at = t0 + i * KP
            h = hits[start + i]
            lists[l0 + n] = table[at]
            lists[l0 + n + 1] = table[at + 1]

            @pl.when(h > 2)
            def _():
                for s in range(2, KP):
                    lists[l0 + n + s] = table[at + s]

            return n + ((h + 1) & 14)

        n = lax.fori_loop(0, TARGETS[which], target, jnp.int32(0))
        start += TARGETS[which]
        filler = ZERO_LEFT | (ZERO_RIGHT[which] << 8)
        for q in range(GROUP):
            lists[l0 + n + q] = filler
        counts[which] = (n + GROUP - 1) // GROUP


def pair_lists(table, hits):
    smem = pl.BlockSpec(memory_space=pltpu.SMEM)
    return pl.pallas_call(
        list_kernel,
        out_shape=(
            jax.ShapeDtypeStruct((LIST_OFF[-1],), jnp.int32),
            jax.ShapeDtypeStruct((6,), jnp.int32),
        ),
        in_specs=[smem, smem],
        out_specs=(smem, smem),
        cost_estimate=pl.CostEstimate(flops=20_000_000, bytes_accessed=40_000_000, transcendentals=0),
        name="pair_lists",
    )(table, hits)


def halves(x):
    hi = x.astype(jnp.bfloat16)
    lo = (x - hi.astype(jnp.float32)).astype(jnp.bfloat16)
    return hi, lo


def put_left(ref, at, hi, lo):
    ref[at, 0:BS, :] = hi
    ref[at, BS : 2 * BS, :] = lo


def put_right(ref, at, hi, lo):
    ref[at, :, 0:BS] = hi
    ref[at, :, BS : 2 * BS] = lo


def each(lo, hi, body, step=4):
    def many(i, _):
        for q in range(step):
            body(lo + i * step + q)
        return 0

    lax.fori_loop(0, (hi - lo) // step, many, 0)


def multiply(which, lists, counts, left, right, total):
    def group(g, _):
        at = LIST_OFF[which] + g * GROUP
        done = []
        for x in range(UNROLL):
            e, f = lists[at + 2 * x], lists[at + 2 * x + 1]
            lhs = jnp.concatenate([left[e & 255], left[f & 255]], axis=1)
            rhs = jnp.concatenate([right[(e >> 8) & 255], right[(f >> 8) & 255]], axis=0)
            r = jnp.dot(lhs, rhs, preferred_element_type=jnp.float32)
            done.append((e >> 16, (r[:BS, :BS] + r[:BS, BS:]) + (r[BS:, :BS] + r[BS:, BS:])))
        for t, q in done:
            total[t] = total[t] + q
        return 0

    lax.fori_loop(0, counts[which], group, 0)


def zero_left(left):
    left[ZERO_LEFT] = jnp.zeros((2 * BS, BS), jnp.bfloat16)


def zero_right(right, which):
    right[ZERO_RIGHT[which]] = jnp.zeros((BS, 2 * BS), jnp.bfloat16)


def near_kernel(
    lists, counts, carry, b1, a1, own, a2, b2, s_out, sp_out, c_out, left_out, stage, left, right, total, s_right, c, sems
):
    loads, at = [], 0
    for i, (src, n) in enumerate(((b1, PIECE), (a1, PIECE), (own, 2 * PIECE), (a2, PIECE), (b2, PIECE))):
        loads.append((pltpu.make_async_copy(src, stage.at[pl.ds(at, n)], sems.at[i]), at, n))
        at += n
    for copy, _, _ in loads:
        copy.start()
    zero_left(left)
    zero_right(right, 0)
    zero_right(s_right, 1)

    def clear(q):
        total[q] = jnp.zeros((BS, BS), jnp.float32)

    each(0, 12 * KS, clear)
    for copy, at, n in loads:
        copy.wait()

        def cut(q):
            hi, lo = halves(stage[q])
            put_left(left, q, hi, lo)
            put_right(right, q, hi, lo)

        each(at, at + n, cut)
    left_copy = pltpu.make_async_copy(left, left_out, sems.at[5])
    left_copy.start()
    multiply(0, lists, counts, left, right, total)
    s_copy = pltpu.make_async_copy(total.at[pl.ds(0, 4 * KS)], s_out, sems.at[6])
    sp_copy = pltpu.make_async_copy(total.at[pl.ds(4 * KS, 8 * KS)], sp_out, sems.at[7])
    s_copy.start()
    sp_copy.start()

    def share(q):
        hi, lo = halves(total[q])
        put_right(s_right, q, hi, lo)

    each(0, 4 * KS, share)

    def begin(q):
        at = carry[q]
        kept = jnp.where(at >= 0, -1.5, 0.0)
        c[q] = kept * total[jnp.maximum(at, 0)]

    each(0, 4 * KC, begin)
    multiply(1, lists, counts, left, s_right, c)
    c_copy = pltpu.make_async_copy(c, c_out, sems.at[8])
    c_copy.start()
    for copy in (left_copy, s_copy, sp_copy, c_copy):
        copy.wait()


def far_kernel(final, lists, counts, below, above, left_in, sp_in, c_in, *refs):
    if final:
        out, stage, left, right, total, s_right, c, sems = refs
    else:
        sp_out, out, stage, left, right, total, s_right, c, sems = refs
    which = 4 if final else 2
    p_copies = (
        pltpu.make_async_copy(below, stage.at[pl.ds(0, PIECE)], sems.at[0]),
        pltpu.make_async_copy(above, stage.at[pl.ds(PIECE, PIECE)], sems.at[1]),
    )
    left_copy = pltpu.make_async_copy(left_in, left, sems.at[2])
    sp_copy = pltpu.make_async_copy(sp_in, total, sems.at[3])
    c_copy = pltpu.make_async_copy(c_in, c, sems.at[4])
    for copy in p_copies + (left_copy, sp_copy, c_copy):
        copy.start()
    zero_right(right, which)
    zero_right(s_right, which + 1)
    for i, copy in enumerate(p_copies):
        copy.wait()

        def cut(q):
            hi, lo = halves(stage[q])
            put_right(right, q, hi, lo)

        each(i * PIECE, (i + 1) * PIECE, cut)
    left_copy.wait()
    sp_copy.wait()
    multiply(which, lists, counts, left, right, total)
    if not final:
        rest = pltpu.make_async_copy(total.at[pl.ds(4 * KS, 4 * KS)], sp_out, sems.at[5])
        rest.start()

    def share(q):
        hi, lo = halves(total[q])
        put_right(s_right, q, hi, lo)

    each(0, 4 * KS, share)
    c_copy.wait()
    multiply(which + 1, lists, counts, left, s_right, c)
    if not final:
        done = pltpu.make_async_copy(c, out, sems.at[6])
        done.start()
        rest.wait()
        done.wait()
        return
    done = []
    for i in range(ROWS):

        def finish(q):
            c[q] = -2.0 * c[q]

        each(i * KC, (i + 1) * KC, finish)
        piece = pl.ds(i * KC, KC)
        done.append(pltpu.make_async_copy(c.at[piece], out.at[piece], sems.at[5 + i]))
        done[-1].start()
    for copy in done:
        copy.wait()


SMEM = pl.BlockSpec(memory_space=pltpu.SMEM)
ANY = pl.BlockSpec(memory_space=pl.ANY)


def f32(n):
    return jax.ShapeDtypeStruct((n, BS, BS), jnp.float32)


def vmem_left():
    return pltpu.VMEM((ZERO_LEFT + 1, 2 * BS, BS), jnp.bfloat16)


def vmem_right(which):
    return pltpu.VMEM((ZERO_RIGHT[which] + 1, BS, 2 * BS), jnp.bfloat16)


def vmem_f32(n):
    return pltpu.VMEM((n, BS, BS), jnp.float32)


def near_step(lists, counts, carry, pieces):
    return pl.pallas_call(
        near_kernel,
        out_shape=(f32(4 * KS), f32(8 * KS), f32(4 * KC), jax.ShapeDtypeStruct((ZERO_LEFT + 1, 2 * BS, BS), jnp.bfloat16)),
        in_specs=[SMEM] * 3 + [ANY] * 5,
        out_specs=(ANY,) * 4,
        scratch_shapes=[
            vmem_f32(12 * KP),
            vmem_left(),
            vmem_right(0),
            vmem_f32(12 * KS),
            vmem_right(1),
            vmem_f32(4 * KC),
            pltpu.SemaphoreType.DMA((9,)),
        ],
        compiler_params=pltpu.CompilerParams(vmem_limit_bytes=48 * 1024 * 1024),
        cost_estimate=pl.CostEstimate(flops=20_000_000_000, bytes_accessed=60_000_000, transcendentals=0),
        name="near_step",
    )(lists, counts, carry, *pieces)


def far_step(final, lists, counts, below, above, left, sp, c):
    rows = 4 if final else 8
    out_shape = f32(4 * KC) if final else (f32(4 * KS), f32(4 * KC))
    return pl.pallas_call(
        functools.partial(far_kernel, final),
        out_shape=out_shape,
        in_specs=[SMEM] * 2 + [ANY] * 5,
        out_specs=ANY if final else (ANY, ANY),
        scratch_shapes=[
            vmem_f32(2 * PIECE),
            vmem_left(),
            vmem_right(2),
            vmem_f32(rows * KS),
            vmem_right(3),
            vmem_f32(4 * KC),
            pltpu.SemaphoreType.DMA((9,)),
        ],
        compiler_params=pltpu.CompilerParams(vmem_limit_bytes=36 * 1024 * 1024),
        cost_estimate=pl.CostEstimate(flops=10_000_000_000, bytes_accessed=40_000_000, transcendentals=0),
        name="last_step" if final else "middle_step",
    )(lists, counts, below, above, left, sp, c)


def local(density, pattern, square_target, cube_target):
    total_rows = ROWS * lax.axis_size(AXES)
    first_row = lax.axis_index(AXES) * ROWS
    base = jnp.remainder(first_row - 2 * ROWS, total_rows).astype(jnp.int32)
    hold = lax.optimization_barrier

    cols = jnp.concatenate([pattern, square_target], axis=1)
    cols_from = [shifted(cols, d) for d in (2, 1, -1, -2)]
    a1 = shifted(density[HALF:].reshape(PIECE, BS, BS), 1)
    a2 = shifted(density[:HALF].reshape(PIECE, BS, BS), -1)
    second, pattern, square_target, cube_target, *cols_from = hold(
        (density, pattern, square_target, cube_target, *cols_from)
    )
    b1 = shifted(second[:HALF].reshape(PIECE, BS, BS), 1)
    b2 = shifted(second[HALF:].reshape(PIECE, BS, BS), -1)
    near = jnp.concatenate(cols_from[:2] + [jnp.concatenate([pattern, square_target], axis=1)] + cols_from[2:], axis=0)
    table, hits, carry = pair_tables(base, near[:, :KP], near[4:16, KP:], cube_target, total_rows)
    a1, a2, table, hits, carry = hold((a1, a2, table, hits, carry))
    c1, c2 = shifted(a1, 1), shifted(a2, -1)
    lists, counts = pair_lists(table, hits)
    b1, b2, lists, counts, carry = hold((b1, b2, lists, counts, carry))
    d1, d2 = shifted(b1, 1), shifted(b2, -1)

    own = density.reshape(2 * PIECE, BS, BS)
    s_own, sp, c, left = near_step(lists, counts, carry, (b1, a1, own, a2, b2))
    sp, c = far_step(False, lists, counts, c1, c2, left, sp, c)
    out = far_step(True, lists, counts, d1, d2, left, sp, c)
    return s_own.reshape(ROWS, KS, BS, BS), out.reshape(ROWS, KC, BS, BS)


def solution(mesh):
    in_specs = (P(AXES, None, None, None), P(AXES, None), P(AXES, None), P(AXES, None))
    out_specs = (P(AXES, None, None, None), P(AXES, None, None, None))
    return jax.shard_map(local, mesh=mesh, in_specs=in_specs, out_specs=out_specs, check_vma=False)
```

time: 469 us -> 128 us (0.27)
  matrix products: 159 us -> 0 us
  waiting for transfers between devices: 122 us -> 0.03 us
  local copies, waits for them, and re-layouts: 130 us -> 10.2 us
  Pallas kernels: 0 us -> 59.4 us
  starting transfers between devices: 29.9 us -> 40 us
  other arithmetic: 24.7 us -> 15.5 us
    dot_general x17 -> x0, matrix products: 159 us -> none  [the longest x8 108 us: one_row(): jnp.einsum('sab,subc->suac', blocks, selected_entries, precision=EXACT_AR...]
    ppermute x8 -> x12, waiting for transfers between devices: 122 us -> 0.03 us  [shifted(): return lax.ppermute(x, AXES, [((i - distance) % n, i) for i in range(n)])]
    gather x16 -> x0, local copies, waits for them, and re-layouts: 62.6 us -> none  [the longest x8 58.2 us: one_row(): selected_entries = jnp.take(right_blocks, slot_rows, axis=0)]
    pallas_call x0 -> x4, Pallas kernels: none -> 59.4 us  [the longest x2 23.1 us: far_step(): pl.pallas_call(functools.partial(far_kernel, final), out_shape=out_shape,...]
    dot_general x8 -> x0, local copies, waits for them, and re-layouts: 58.1 us -> none  [one_row(): jnp.einsum('sab,subc->suac', blocks, selected_entries, precision=EXACT_AR...]
    concatenate x4 -> x3, other arithmetic: 15.8 us -> 2.34 us  [the longest x1 0.79 us: local(): cols = jnp.concatenate([pattern, square_target], axis=1)]
    ppermute x8 -> x12, starting transfers between devices: 29.9 us -> 40 us  [shifted(): return lax.ppermute(x, AXES, [((i - distance) % n, i) for i in range(n)])]
    unnamed x8 -> x19, local copies, waits for them, and re-layouts: 9.33 us -> 1.4 us
  transfers between devices with their start and end apart: 8 -> 12, of which waited for: 2 -> 0; matrix products, arithmetic and copies ran while one was open for 1% -> 19% of each run, Pallas kernels for 0% -> 39%
where the time goes in v2:
time: 128 us; the launch traced here: 126 us
  Pallas kernels  59.4 us (46%)
  starting transfers between devices  40 us (31%)
  other arithmetic  15.5 us (12%)
  local copies, waits for them, and re-layouts  10.2 us (8%)
  between operations  1.34 us (1%)
    ppermute x12, starting transfers between devices, shifted(): return lax.ppermute(x, AXES, [((i - distance) % n, i) for i in range(n)])  40 us
    pallas_call x2, Pallas kernels, far_step(): pl.pallas_call(functools.partial(far_kernel, final), out_shape=out_shape,...  23.1 us
    pallas_call x1, Pallas kernels, near_step(): pl.pallas_call(near_kernel, out_shape=(f32(4 * KS), f32(8 * KS), f32(4 *...  20.4 us
    pallas_call x1, Pallas kernels, pair_lists(): pl.pallas_call(list_kernel, out_shape=(jax.ShapeDtypeStruct((LIST_OFF[-1]...  15.9 us
    reduce_sum x6, other arithmetic, pick(): return jnp.sum(jnp.where(hot.reshape(shape), table, 0), axis=index.ndim)  5.66 us
    slice x1, local copies, waits for them, and re-layouts, local(): a2 = shifted(density[:HALF].reshape(PIECE, BS, BS), -1)  3.12 us
    slice x1, local copies, waits for them, and re-layouts, local(): b2 = shifted(second[HALF:].reshape(PIECE, BS, BS), -1)  3.08 us
  transfers between devices with their start and end apart: 12, of which 0 were waited for; matrix products, arithmetic and copies ran while one was open for 19% of the time, Pallas kernels for 39%

profile of v2, /device:TPU:0, one launch (start us, length us, event | category | flops | bytes accessed | tf_op | source)
XLA Modules:
  0.0 126.5 jit_solution(15996755989637268363)
XLA Ops:
  0.7 0.8 pad_add_fusion.4
  1.5 8.4 %collective-permute-start.3 = (s32[4,24]{1,0:T(4,128)S(1)}, s32[4,24]{1,0:T(4,128)S(1)}, u32[]{:S(2)}, u32[]{:S(2)}) collective-permute-start(s32[4,24]{1,0:T(4,128)S(1)} %pad_add_fusion.4), channel_id=1, source_target_pairs={{2,0},{3,1},{4,2},{5,3},{6,4},{7,5},{8,6},{9,7},{10,8},{11,9},{12,... | collective-permute-start | bytes 1160 | tf_op jit(solution)/shard_map/ppermute | solution.py:30
  9.9 0.8 collective-permute-start.2
  10.6 1.3 collective-permute-start.1
  11.9 0.7 collective-permute-start
  12.6 3.1 %fusion.6 = (f32[2,8,128,128]{3,2,1,0:T(8,128)}, f32[2,8,128,128]{3,2,1,0:T(8,128)}) fusion(f32[4,8,128,128]{3,2,1,0:T(8,128)} %param.22), kind=kLoop, calls=%fused_computation.87 | loop fusion | bytes 4194304 | tf_op jit(solution)/shard_map/slice | solution.py:373
  15.8 7.2 %collective-permute-start.7 = (f32[16,128,128]{2,1,0:T(8,128)}, f32[16,128,128]{2,1,0:T(8,128)S(1)}, u32[]{:S(2)}, u32[]{:S(2)}) collective-permute-start(f32[16,128,128]{2,1,0:T(8,128)} %bitcast.3), channel_id=1, source_target_pairs={{1,0},{2,1},{3,2},{4,3},{5,4},{6,5},{7,6},{8,7},{9,8},{10,9},{11,1... | collective-permute-start | bytes 3145736 | tf_op jit(solution)/shard_map/ppermute | solution.py:30
  23.0 0.7 broadcast_compare_fusion.8
  23.7 0.7 fusion.5
  24.5 1.0 select_reduce_fusion.9
  25.6 0.8 pad_add_fusion.5
  26.4 0.8 pad_add_fusion.2
  27.3 0.9 select_reduce_fusion.10
  28.3 0.9 select_reduce_fusion.8
  29.3 1.0 select_reduce_fusion.6
  30.4 0.7 broadcast_compare_fusion.5
  31.1 0.8 select_reduce_fusion.7
  32.2 1.7 %select_reduce_fusion.1 = s32[12,8,8]{2,1,0:T(8,128)S(1)} fusion(s32[20,8]{0,1:T(8,128)S(1)} %copy.53, pred[12,8,20]{2,1,0:T(8,128)(4,1)S(1)} %iota_compare_fusion.2), kind=kLoop, calls=%fused_computation.1 | loop fusion | flops 29952 | bytes 5632 | tf_op jit(solution)/shard_map/reduce_sum | solution.py:51
  34.9 0.8 shift-left_or_fusion.3
  35.7 0.8 shift-left_or_fusion.1
  36.6 0.8 shift-left_or_fusion
  37.5 3.1 %fusion.7 = (f32[2,8,128,128]{3,2,1,0:T(8,128)}, f32[2,8,128,128]{3,2,1,0:T(8,128)}) fusion(f32[4,8,128,128]{3,2,1,0:T(8,128)} %param.22), kind=kLoop, calls=%fused_computation.88 | loop fusion | bytes 4194304 | tf_op jit(solution)/shard_map/slice | solution.py:378
  40.6 7.2 %collective-permute-start.5 = (f32[16,128,128]{2,1,0:T(8,128)}, f32[16,128,128]{2,1,0:T(8,128)}, u32[]{:S(2)}, u32[]{:S(2)}) collective-permute-start(f32[16,128,128]{2,1,0:T(8,128)} %bitcast.1), channel_id=1, source_target_pairs={{1,0},{2,1},{3,2},{4,3},{5,4},{6,5},{7,6},{8,7},{9,8},{10,9},{11,1... | collective-permute-start | bytes 3145736 | tf_op jit(solution)/shard_map/ppermute | solution.py:30
  50.2 0.8 select_n.147.table
  51.0 7.2 %collective-permute-start.11 = (f32[16,128,128]{2,1,0:T(8,128)S(1)}, f32[16,128,128]{2,1,0:T(8,128)}, u32[]{:S(2)}, u32[]{:S(2)}) collective-permute-start(f32[16,128,128]{2,1,0:T(8,128)S(1)} %collective-permute-done.7.a2), channel_id=1, source_target_pairs={{1,0},{2,1},{3,2},{4,3},{5,4},{6,5},{7,6},{8,7},{9,8},{10,9},{11,1... | collective-permute-start | bytes 3145736 | tf_op jit(solution)/shard_map/ppermute | solution.py:30
  58.2 15.9 %pair_lists.1 = (s32[5472]{0:T(1024)}, s32[6]{0:T(128)}) custom-call(s32[5376]{0:T(1024)} %select_n.147.table, s32[672]{0:T(1024)} %get-tuple-element.37.hits), custom_call_target="tpu_custom_call" | custom-call | flops 20000000 | bytes 40000000 | tf_op jit(solution)/shard_map/pair_lists/pallas_call | solution.py:125
  74.2 7.2 %collective-permute-start.9 = (f32[16,128,128]{2,1,0:T(8,128)}, f32[16,128,128]{2,1,0:T(8,128)S(1)}, u32[]{:S(2)}, u32[]{:S(2)}) collective-permute-start(f32[16,128,128]{2,1,0:T(8,128)} %collective-permute-done.5.b2), channel_id=1, source_target_pairs={{1,0},{2,1},{3,2},{4,3},{5,4},{6,5},{7,6},{8,7},{9,8},{10,9},{11,1... | collective-permute-start | bytes 3145736 | tf_op jit(solution)/shard_map/ppermute | solution.py:30
  81.4 0.7 copy-done
  82.1 0.6 copy-done.2
  82.7 20.4 %near_step.1 = (f32[64,128,128]{2,1,0:T(8,128)}, f32[128,128,128]{2,1,0:T(8,128)}, f32[96,128,128]{2,1,0:T(8,128)}, bf16[97,256,128]{2,1,0:T(8,128)(2,1)}) custom-call(s32[5472]{0:T(1024)S(1)} %copy-done, s32[6]{0:T(128)S(1)} %copy-done.2, s32[96]{0:T(128)S(1)} %select_n.150.carry, f32[16,128,128]{2,1,0:T(8,128)S(1)} %collective-permute-done.4.b1, ...), custom_call_target="tpu_custom_call" | custom-call | flops 20000000000 | bytes 60000000 | tf_op jit(solution)/shard_map/near_step/pallas_call | solution.py:321
  103.2 12.9 %middle_step.1 = (f32[64,128,128]{2,1,0:T(8,128)S(1)}, f32[96,128,128]{2,1,0:T(8,128)S(1)}) custom-call(s32[5472]{0:T(1024)S(1)} %copy-done.1, s32[6]{0:T(128)S(1)} %copy-done.3, f32[16,128,128]{2,1,0:T(8,128)} %collective-permute-done.10.below, f32[16,128,128]{2,1,0:T(8,128)} %collective-permute-done.11.above, ...), custom_call_target="tpu_custom_call" | custom-call | flops 10000000000 | bytes 40000000 | tf_op jit(solution)/shard_map/middle_step/pallas_call | solution.py:344
  116.1 10.2 %last_step.1 = f32[96,128,128]{2,1,0:T(8,128)} custom-call(s32[5472]{0:T(1024)S(1)} %copy-done.1, s32[6]{0:T(128)S(1)} %copy-done.3, f32[16,128,128]{2,1,0:T(8,128)S(1)} %collective-permute-done.8.below, f32[16,128,128]{2,1,0:T(8,128)S(1)} %collective-permute-done.9.above, bf16[97,256,128]{2,1,0:T(8,128)(2,1)} %get-tuple-element.49.left_in, ...), custom_call_target="tpu_custom_call" | custom-call | flops 10000000000 | bytes 40000000 | tf_op jit(solution)/shard_map/last_step/pallas_call | solution.py:344
  (110 shorter events, 4.5 us)
Async XLA Ops:
  0.6 47.6 %copy-start.6 = (s32[4,8]{1,0:T(4,128)S(1)}, s32[4,8]{1,0:T(4,128)}, u32[]{:S(2)}) copy-start(s32[4,8]{1,0:T(4,128)} %constant.127.clone) | copy-start | bytes 388
  0.6 49.1 %copy-start.7 = (pred[8,8]{1,0:T(8,128)(4,1)S(1)}, pred[8,8]{1,0:T(8,128)(4,1)}, u32[]{:S(2)}) copy-start(pred[8,8]{1,0:T(8,128)(4,1)} %constant.148) | copy-start | bytes 196
  0.7 49.4 %copy-start.5 = (s32[672]{0:T(1024)S(1)}, s32[672]{0:T(1024)}, u32[]{:S(2)}) copy-start(s32[672]{0:T(1024)} %constant.135.clone) | copy-start | bytes 8068
  0.7 47.1 %copy-start.4 = (s32[4,24]{1,0:T(4,128)S(1)}, s32[4,24]{1,0:T(4,128)}, u32[]{:S(2)}) copy-start(s32[4,24]{1,0:T(4,128)} %param.25) | copy-start | bytes 1156
  1.5 14.3 %collective-permute-start.3 = (s32[4,24]{1,0:T(4,128)S(1)}, s32[4,24]{1,0:T(4,128)S(1)}, u32[]{:S(2)}, u32[]{:S(2)}) collective-permute-start(s32[4,24]{1,0:T(4,128)S(1)} %pad_add_fusion.4), channel_id=1, source_target_pairs={{2,0},{3,1},{4,2},{5,3},{6,4},{7,5},{8,6},{9,7},{10,8},{11,9},{12,... | collective-permute-start | bytes 1160 | tf_op jit(solution)/shard_map/ppermute | solution.py:30
  9.9 13.2 %collective-permute-start.2 = (s32[4,24]{1,0:T(4,128)S(1)}, s32[4,24]{1,0:T(4,128)S(1)}, u32[]{:S(2)}, u32[]{:S(2)}) collective-permute-start(s32[4,24]{1,0:T(4,128)S(1)} %pad_add_fusion.4), channel_id=1, source_target_pairs={{1,0},{2,1},{3,2},{4,3},{5,4},{6,5},{7,6},{8,7},{9,8},{10,9},{11,1... | collective-permute-start | bytes 1160 | tf_op jit(solution)/shard_map/ppermute | solution.py:30
  10.6 12.4 %collective-permute-start.1 = (s32[4,24]{1,0:T(4,128)S(1)}, s32[4,24]{1,0:T(4,128)S(1)}, u32[]{:S(2)}, u32[]{:S(2)}) collective-permute-start(s32[4,24]{1,0:T(4,128)S(1)} %pad_add_fusion.4), channel_id=1, source_target_pairs={{255,0},{0,1},{1,2},{2,3},{3,4},{4,5},{5,6},{6,7},{7,8},{8,9},{9,1... | collective-permute-start | bytes 1160 | tf_op jit(solution)/shard_map/ppermute | solution.py:30
  11.9 11.2 %collective-permute-start = (s32[4,24]{1,0:T(4,128)S(1)}, s32[4,24]{1,0:T(4,128)S(1)}, u32[]{:S(2)}, u32[]{:S(2)}) collective-permute-start(s32[4,24]{1,0:T(4,128)S(1)} %pad_add_fusion.4), channel_id=1, source_target_pairs={{254,0},{255,1},{0,2},{1,3},{2,4},{3,5},{4,6},{5,7},{6,8},{7,9},{8... | collective-permute-start | bytes 1160 | tf_op jit(solution)/shard_map/ppermute | solution.py:30
  15.7 35.3 %collective-permute-start.6 = (f32[16,128,128]{2,1,0:T(8,128)}, f32[16,128,128]{2,1,0:T(8,128)S(1)}, u32[]{:S(2)}, u32[]{:S(2)}) collective-permute-start(f32[16,128,128]{2,1,0:T(8,128)} %bitcast.2), channel_id=1, source_target_pairs={{255,0},{0,1},{1,2},{2,3},{3,4},{4,5},{5,6},{6,7},{7,8},{8,9},{9,1... | collective-permute-start | bytes 3145736 | tf_op jit(solution)/shard_map/ppermute | solution.py:30
  15.8 35.2 %collective-permute-start.7 = (f32[16,128,128]{2,1,0:T(8,128)}, f32[16,128,128]{2,1,0:T(8,128)S(1)}, u32[]{:S(2)}, u32[]{:S(2)}) collective-permute-start(f32[16,128,128]{2,1,0:T(8,128)} %bitcast.3), channel_id=1, source_target_pairs={{1,0},{2,1},{3,2},{4,3},{5,4},{6,5},{7,6},{8,7},{9,8},{10,9},{11,1... | collective-permute-start | bytes 3145736 | tf_op jit(solution)/shard_map/ppermute | solution.py:30
  40.6 33.5 %collective-permute-start.4 = (f32[16,128,128]{2,1,0:T(8,128)}, f32[16,128,128]{2,1,0:T(8,128)S(1)}, u32[]{:S(2)}, u32[]{:S(2)}) collective-permute-start(f32[16,128,128]{2,1,0:T(8,128)} %bitcast), channel_id=1, source_target_pairs={{255,0},{0,1},{1,2},{2,3},{3,4},{4,5},{5,6},{6,7},{7,8},{8,9},{9,1... | collective-permute-start | bytes 3145736 | tf_op jit(solution)/shard_map/ppermute | solution.py:30
  40.6 33.5 %collective-permute-start.5 = (f32[16,128,128]{2,1,0:T(8,128)}, f32[16,128,128]{2,1,0:T(8,128)}, u32[]{:S(2)}, u32[]{:S(2)}) collective-permute-start(f32[16,128,128]{2,1,0:T(8,128)} %bitcast.1), channel_id=1, source_target_pairs={{1,0},{2,1},{3,2},{4,3},{5,4},{6,5},{7,6},{8,7},{9,8},{10,9},{11,1... | collective-permute-start | bytes 3145736 | tf_op jit(solution)/shard_map/ppermute | solution.py:30
  51.0 52.1 %collective-permute-start.10 = (f32[16,128,128]{2,1,0:T(8,128)S(1)}, f32[16,128,128]{2,1,0:T(8,128)}, u32[]{:S(2)}, u32[]{:S(2)}) collective-permute-start(f32[16,128,128]{2,1,0:T(8,128)S(1)} %collective-permute-done.6.a1), channel_id=1, source_target_pairs={{255,0},{0,1},{1,2},{2,3},{3,4},{4,5},{5,6},{6,7},{7,8},{8,9},{9,1... | collective-permute-start | bytes 3145736 | tf_op jit(solution)/shard_map/ppermute | solution.py:30
  51.0 52.1 %collective-permute-start.11 = (f32[16,128,128]{2,1,0:T(8,128)S(1)}, f32[16,128,128]{2,1,0:T(8,128)}, u32[]{:S(2)}, u32[]{:S(2)}) collective-permute-start(f32[16,128,128]{2,1,0:T(8,128)S(1)} %collective-permute-done.7.a2), channel_id=1, source_target_pairs={{1,0},{2,1},{3,2},{4,3},{5,4},{6,5},{7,6},{8,7},{9,8},{10,9},{11,1... | collective-permute-start | bytes 3145736 | tf_op jit(solution)/shard_map/ppermute | solution.py:30
  74.1 42.0 %collective-permute-start.8 = (f32[16,128,128]{2,1,0:T(8,128)S(1)}, f32[16,128,128]{2,1,0:T(8,128)S(1)}, u32[]{:S(2)}, u32[]{:S(2)}) collective-permute-start(f32[16,128,128]{2,1,0:T(8,128)S(1)} %collective-permute-done.4.b1), channel_id=1, source_target_pairs={{255,0},{0,1},{1,2},{2,3},{3,4},{4,5},{5,6},{6,7},{7,8},{8,9},{9,1... | collective-permute-start | bytes 3145736 | tf_op jit(solution)/shard_map/ppermute | solution.py:30
  74.2 41.9 %collective-permute-start.9 = (f32[16,128,128]{2,1,0:T(8,128)}, f32[16,128,128]{2,1,0:T(8,128)S(1)}, u32[]{:S(2)}, u32[]{:S(2)}) collective-permute-start(f32[16,128,128]{2,1,0:T(8,128)} %collective-permute-done.5.b2), channel_id=1, source_target_pairs={{1,0},{2,1},{3,2},{4,3},{5,4},{6,5},{7,6},{8,7},{9,8},{10,9},{11,1... | collective-permute-start | bytes 3145736 | tf_op jit(solution)/shard_map/ppermute | solution.py:30
  81.4 0.7 copy-start
  82.1 0.6 copy-start.2
  82.7 20.4 %copy-start.1 = (s32[5472]{0:T(1024)S(1)}, s32[5472]{0:T(1024)}, u32[]{:S(2)}) copy-start(s32[5472]{0:T(1024)} %get-tuple-element.41.lists) | copy-start | bytes 65668
  82.7 20.4 %copy-start.3 = (s32[6]{0:T(128)S(1)}, s32[6]{0:T(128)}, u32[]{:S(2)}) copy-start(s32[6]{0:T(128)} %get-tuple-element.42.counts) | copy-start | bytes 76

commit v3 on v2

v3 whole, which is shorter than its diff:
```python
import functools

import jax
import jax.numpy as jnp
import numpy as np
from jax import lax
from jax.experimental import pallas as pl
from jax.experimental.pallas import tpu as pltpu
from jax.sharding import PartitionSpec as P

AXES = ("row", "col")
ROWS, KP, KS, KC, BS = 4, 8, 16, 24, 128
HALF = ROWS // 2
PIECE = HALF * KP
GROUP = 16
ZERO_LEFT = 12 * KP

OWN, MIDDLE, LAST = (4, 5, 6, 7), (2, 3, 8, 9), (0, 1, 10, 11)
ORDER = OWN + MIDDLE + LAST

TARGETS = (12 * KS, 4 * KC, 8 * KS, 4 * KC, 4 * KS, 4 * KC)
ZERO_RIGHT = (12 * KP, 4 * KS, 2 * PIECE, 4 * KS, 2 * PIECE, 4 * KS)
TABLE_OFF = tuple(int(x) for x in np.cumsum((0,) + tuple(t * KP for t in TARGETS)))
LIST_OFF = tuple(int(x) for x in np.cumsum((0,) + tuple(t * KP + GROUP for t in TARGETS)))


def shifted(x, distance):
    n = lax.axis_size(AXES)
    return lax.ppermute(x, AXES, [((i - distance) % n, i) for i in range(n)])


def lookup(rows, count):
    table = np.full((count,), -1, np.int32)
    table[list(rows)] = np.arange(len(rows))
    return table


def pair_tables(base, pat20, sq12, cu4, total_rows):
    def place(cols, start, count):
        return jnp.minimum(jnp.remainder(cols - start, total_rows), count - 1)

    def matched(left_cols, right_cols, targets):
        same = right_cols[:, None, :, :] == targets[:, :, None, None]
        same = same & (targets >= 0)[:, :, None, None] & (left_cols >= 0)[:, None, :, None]
        return jnp.max(jnp.where(same, jnp.arange(right_cols.shape[-1], dtype=jnp.int32), -1), axis=-1)

    def pick(table, index):
        hot = index[..., None] == jnp.arange(table.shape[0], dtype=jnp.int32)
        shape = hot.shape + (1,) * (table.ndim - 1)
        return jnp.sum(jnp.where(hot.reshape(shape), table, 0), axis=index.ndim)

    def entries(u, left, right_row, width, target):
        right = right_row[:, None, :] * width + u
        ok = (u >= 0) & (right_row >= 0)[:, None, :]
        return jnp.where(ok, left[:, None, :] | (right << 8) | (target[:, :, None] << 16), -1).reshape(-1, KP)

    def const(x):
        return jnp.asarray(np.asarray(x, np.int32))

    slots = np.arange(KP, dtype=np.int32)
    near_p = lookup(range(4, 16), 20)
    mid_p = lookup((2, 3, 16, 17), 20)
    last_p = lookup((0, 1, 18, 19), 20)

    pk = pat20[4:16]
    at = place(pk, base, 20)
    u = matched(pk, pick(pat20, at), sq12)
    pi = pat20[8:12]
    pi_at = place(pi, base + 4, 12)
    in_pattern = jnp.any((pi_at[:, :, None] == const(np.arange(12))) & (pi >= 0)[:, :, None], axis=1)
    in_cube = jnp.any(sq12[None, :, :, None] == cu4[:, None, None, :], axis=-1)
    used = jnp.any(in_pattern[:, :, None] & in_cube, axis=0) | const(lookup(OWN, 12) >= 0).astype(bool)[:, None]
    u = jnp.where(used[:, :, None], u, -1)
    tables = {}
    for which, (rows, here) in enumerate(((ORDER, near_p), (MIDDLE + LAST, mid_p), (LAST, last_p))):
        sel = np.asarray(rows)
        target = const(np.arange(len(rows))[:, None] * KS + np.arange(KS))
        take = lambda x: jnp.stack([x[r] for r in rows])
        tables[2 * which] = entries(take(u), const(np.arange(12)[sel][:, None] * KP + slots), pick(const(here), take(at)), KP, target)

    at = pi_at
    u = matched(pi, pick(sq12, at), cu4)
    left = const((np.arange(4) + 4)[:, None] * KP + slots)
    target = const(np.arange(4)[:, None] * KC + np.arange(KC))
    for which, rows in enumerate((OWN, MIDDLE, LAST)):
        tables[2 * which + 1] = entries(u, left, pick(const(lookup(rows, 12)), at), KS, target)

    same = (cu4[:, :, None] == sq12[4:8][:, None, :]) & (cu4 >= 0)[:, :, None]
    slot = jnp.max(jnp.where(same, jnp.arange(KS, dtype=jnp.int32), -1), axis=-1)
    carry = jnp.where(slot >= 0, slot + const(np.arange(4)[:, None] * KS), -1).reshape(-1)
    table = jnp.concatenate([tables[i] for i in range(6)])
    hit = table >= 0
    rank = jnp.sum(jnp.where(hit[:, None, :] & (slots[None, :] < slots[:, None])[None], 1, 0), axis=-1)
    moved = hit[:, None, :] & (rank[:, None, :] == slots[None, :, None])
    packed = jnp.sum(jnp.where(moved, table[:, None, :], 0), axis=-1)
    return packed.reshape(-1), jnp.sum(hit.astype(jnp.int32), axis=-1), carry


def list_kernel(table, hits, lists, counts):
    start = 0
    for which in range(6):
        t0, l0 = TABLE_OFF[which], LIST_OFF[which]

        def targets(i, n):
            first = i * 4
            h = [hits[start + first + q] for q in range(4)]
            at = [n]
            for q in range(4):
                at.append(at[-1] + h[q])
            e = [[table[t0 + (first + q) * KP + s] for s in range(4)] for q in range(4)]
            for q in range(4):
                for s in range(4):
                    lists[l0 + at[q] + s] = e[q][s]

                @pl.when(h[q] > 4)
                def _():
                    for s in range(4, KP):
                        lists[l0 + at[q] + s] = table[t0 + (first + q) * KP + s]

            return at[4]

        n = lax.fori_loop(0, TARGETS[which] // 4, targets, jnp.int32(0))
        start += TARGETS[which]
        filler = ZERO_LEFT | (ZERO_RIGHT[which] << 8)
        for q in range(GROUP):
            lists[l0 + n + q] = filler
        counts[which] = (n + GROUP - 1) // GROUP


def pair_lists(table, hits):
    smem = pl.BlockSpec(memory_space=pltpu.SMEM)
    return pl.pallas_call(
        list_kernel,
        out_shape=(
            jax.ShapeDtypeStruct((LIST_OFF[-1],), jnp.int32),
            jax.ShapeDtypeStruct((6,), jnp.int32),
        ),
        in_specs=[smem, smem],
        out_specs=(smem, smem),
        cost_estimate=pl.CostEstimate(flops=20_000_000, bytes_accessed=40_000_000, transcendentals=0),
        name="pair_lists",
    )(table, hits)


def halves(x):
    hi = x.astype(jnp.bfloat16)
    lo = (x - hi.astype(jnp.float32)).astype(jnp.bfloat16)
    return hi, lo


def put(ref, at, x):
    hi, lo = halves(x)
    ref[at, :, 0:BS] = hi
    ref[at, :, BS : 2 * BS] = lo


def each(lo, hi, body, step=4):
    def many(i, _):
        for q in range(step):
            body(lo + i * step + q)
        return 0

    lax.fori_loop(0, (hi - lo) // step, many, 0)


def multiply(which, lists, counts, left, right, total, scale=None):
    def group(g, _):
        at = LIST_OFF[which] + g * GROUP
        none = jnp.zeros((BS, BS), jnp.bfloat16)
        done = []
        for x in range(GROUP):
            e = lists[at + x]
            b = right[(e >> 8) & 255]
            rhs = jnp.concatenate([b, jnp.concatenate([b[:, :BS], none], axis=1)], axis=0)
            r = jnp.dot(left[e & 255], rhs, preferred_element_type=jnp.float32)
            done.append((e >> 16, r[:, :BS] + r[:, BS:]))
        for t, q in done:
            total[t] = total[t] + (q if scale is None else scale * q)
        return 0

    lax.fori_loop(0, counts[which], group, 0)


def zero(ref, at):
    ref[at] = jnp.zeros((BS, 2 * BS), jnp.bfloat16)


def near_kernel(lists, counts, carry, b1, a1, own, a2, b2, s_out, sp_out, c_out, cut_out, stage, cut, total, s_cut, c, sems):
    loads = []
    for i, (src, at, n) in enumerate(
        ((own, 2, 2), (a1, 1, 1), (a2, 4, 1), (b1, 0, 1), (b2, 5, 1))
    ):
        at, n = at * PIECE, n * PIECE
        loads.append((pltpu.make_async_copy(src, stage.at[pl.ds(at, n)], sems.at[i]), at, n))
    for copy, _, _ in loads:
        copy.start()
    zero(cut, ZERO_LEFT)
    zero(s_cut, 4 * KS)

    def clear(q):
        total[q] = jnp.zeros((BS, BS), jnp.float32)

    each(0, 12 * KS, clear)
    for copy, at, n in loads:
        copy.wait()
        each(at, at + n, lambda q: put(cut, q, stage[q]))
    cut_copy = pltpu.make_async_copy(cut, cut_out, sems.at[5])
    cut_copy.start()
    multiply(0, lists, counts, cut, cut, total)
    s_copy = pltpu.make_async_copy(total.at[pl.ds(0, 4 * KS)], s_out, sems.at[6])
    sp_copy = pltpu.make_async_copy(total.at[pl.ds(4 * KS, 8 * KS)], sp_out, sems.at[7])
    s_copy.start()
    sp_copy.start()
    each(0, 4 * KS, lambda q: put(s_cut, q, total[q]))

    def begin(q):
        at = carry[q]
        kept = jnp.where(at >= 0, -1.5, 0.0)
        c[q] = kept * total[jnp.maximum(at, 0)]

    each(0, 4 * KC, begin)
    multiply(1, lists, counts, cut, s_cut, c)
    c_copy = pltpu.make_async_copy(c, c_out, sems.at[8])
    c_copy.start()
    for copy in (cut_copy, s_copy, sp_copy, c_copy):
        copy.wait()


def far_kernel(final, lists, counts, below, above, left_in, sp_in, c_in, *refs):
    if final:
        out, stage, left, right, sp, s_cut, c, sems = refs
    else:
        sp_out, out, stage, left, right, sp, s_cut, c, sems = refs
    which = 4 if final else 2
    loads = [
        pltpu.make_async_copy(below, stage.at[pl.ds(0, PIECE)], sems.at[0]),
        pltpu.make_async_copy(above, stage.at[pl.ds(PIECE, PIECE)], sems.at[1]),
    ]
    ranges = ((0, 2 * KP), (10 * KP, 2 * KP + 1)) if final else ((0, 4 * KP), (8 * KP, 4 * KP + 1))
    for i, (at, n) in enumerate(ranges + ((4 * KP, 4 * KP),)):
        loads.append(pltpu.make_async_copy(left_in.at[pl.ds(at, n)], left.at[pl.ds(at, n)], sems.at[2 + i]))
    own_left = loads.pop()
    loads.append(pltpu.make_async_copy(sp_in, sp, sems.at[5]))
    c_copy = pltpu.make_async_copy(c_in, c, sems.at[6])
    for copy in loads + [own_left, c_copy]:
        copy.start()
    zero(right, 2 * PIECE)
    zero(s_cut, 4 * KS)
    for i, copy in enumerate(loads[:2]):
        copy.wait()
        each(i * PIECE, (i + 1) * PIECE, lambda q: put(right, q, stage[q]))
    for copy in loads[2:]:
        copy.wait()
    multiply(which, lists, counts, left, right, sp)
    done = []
    if not final:
        done.append(pltpu.make_async_copy(sp.at[pl.ds(4 * KS, 4 * KS)], sp_out, sems.at[7]))
        done[-1].start()
    each(0, 4 * KS, lambda q: put(s_cut, q, sp[q]))
    own_left.wait()
    c_copy.wait()
    multiply(which + 1, lists, counts, left, s_cut, c, scale=-2.0 if final else None)
    for i in range(ROWS):
        if not final:

            def finish(q):
                c[q] = -2.0 * c[q]

            each(i * KC, (i + 1) * KC, finish)
        piece = pl.ds(i * KC, KC)
        done.append(pltpu.make_async_copy(c.at[piece], out.at[piece], sems.at[8 + i]))
        done[-1].start()
    for copy in done:
        copy.wait()


SMEM = pl.BlockSpec(memory_space=pltpu.SMEM)
ANY = pl.BlockSpec(memory_space=pl.ANY)
VMEM = pl.BlockSpec(memory_space=pltpu.VMEM)


def f32(n):
    return jax.ShapeDtypeStruct((n, BS, BS), jnp.float32)


def vmem_cut(n):
    return pltpu.VMEM((n + 1, BS, 2 * BS), jnp.bfloat16)


def vmem_f32(n):
    return pltpu.VMEM((n, BS, BS), jnp.float32)


def near_step(lists, counts, carry, pieces):
    return pl.pallas_call(
        near_kernel,
        out_shape=(
            f32(4 * KS),
            f32(8 * KS),
            f32(4 * KC),
            jax.ShapeDtypeStruct((ZERO_LEFT + 1, BS, 2 * BS), jnp.bfloat16),
        ),
        in_specs=[SMEM] * 3 + [ANY] * 5,
        out_specs=(ANY,) * 4,
        scratch_shapes=[
            vmem_f32(12 * KP),
            vmem_cut(ZERO_LEFT),
            vmem_f32(12 * KS),
            vmem_cut(4 * KS),
            vmem_f32(4 * KC),
            pltpu.SemaphoreType.DMA((9,)),
        ],
        compiler_params=pltpu.CompilerParams(vmem_limit_bytes=48 * 1024 * 1024),
        cost_estimate=pl.CostEstimate(flops=20_000_000_000, bytes_accessed=60_000_000, transcendentals=0),
        name="near_step",
    )(lists, counts, carry, *pieces)


def far_step(final, lists, counts, below, above, left, sp, c):
    return pl.pallas_call(
        functools.partial(far_kernel, final),
        out_shape=f32(4 * KC) if final else (f32(4 * KS), f32(4 * KC)),
        in_specs=[SMEM] * 2 + [ANY] * 5,
        out_specs=ANY if final else (ANY, ANY),
        scratch_shapes=[
            vmem_f32(2 * PIECE),
            vmem_cut(ZERO_LEFT),
            vmem_cut(2 * PIECE),
            vmem_f32((4 if final else 8) * KS),
            vmem_cut(4 * KS),
            vmem_f32(4 * KC),
            pltpu.SemaphoreType.DMA((12,)),
        ],
        compiler_params=pltpu.CompilerParams(vmem_limit_bytes=36 * 1024 * 1024),
        cost_estimate=pl.CostEstimate(flops=10_000_000_000, bytes_accessed=40_000_000, transcendentals=0),
        name="last_step" if final else "middle_step",
    )(lists, counts, below, above, left, sp, c)


def split_kernel(src, one, two, sems):
    copies = [
        pltpu.make_async_copy(src.at[pl.ds(i * PIECE, PIECE)], dst, sems.at[i]) for i, dst in enumerate((one, two))
    ]
    for copy in copies:
        copy.start()
    for copy in copies:
        copy.wait()


def split(blocks):
    return pl.pallas_call(
        split_kernel,
        out_shape=(vmem_f32(PIECE), vmem_f32(PIECE)),
        in_specs=[ANY],
        out_specs=(VMEM, VMEM),
        scratch_shapes=[pltpu.SemaphoreType.DMA((2,))],
        cost_estimate=pl.CostEstimate(flops=0, bytes_accessed=4_000_000, transcendentals=0),
        name="split",
    )(blocks)


def local(density, pattern, square_target, cube_target):
    total_rows = ROWS * lax.axis_size(AXES)
    first_row = lax.axis_index(AXES) * ROWS
    base = jnp.remainder(first_row - 2 * ROWS, total_rows).astype(jnp.int32)
    hold = lax.optimization_barrier

    cols = jnp.concatenate([pattern, square_target], axis=1)
    cols_from = [shifted(cols, d) for d in (2, 1, -1, -2)]
    own = density.reshape(2 * PIECE, BS, BS)
    lower, upper = split(own)
    a1, a2 = shifted(upper, 1), shifted(lower, -1)
    lower, upper, pattern, square_target, cube_target, *cols_from = hold(
        (lower, upper, pattern, square_target, cube_target, *cols_from)
    )
    b1, b2 = shifted(lower, 1), shifted(upper, -1)
    near = jnp.concatenate(cols_from[:2] + [jnp.concatenate([pattern, square_target], axis=1)] + cols_from[2:], axis=0)
    table, hits, carry = pair_tables(base, near[:, :KP], near[4:16, KP:], cube_target, total_rows)
    a1, a2, table, hits, carry = hold((a1, a2, table, hits, carry))
    c1, c2 = shifted(a1, 1), shifted(a2, -1)
    lists, counts = pair_lists(table, hits)
    b1, b2, lists, counts, carry = hold((b1, b2, lists, counts, carry))
    d1, d2 = shifted(b1, 1), shifted(b2, -1)

    s_own, sp, c, left = near_step(lists, counts, carry, (b1, a1, own, a2, b2))
    sp, c = far_step(False, lists, counts, c1, c2, left, sp, c)
    out = far_step(True, lists, counts, d1, d2, left, sp, c)
    return s_own.reshape(ROWS, KS, BS, BS), out.reshape(ROWS, KC, BS, BS)


def solution(mesh):
    in_specs = (P(AXES, None, None, None), P(AXES, None), P(AXES, None), P(AXES, None))
    out_specs = (P(AXES, None, None, None), P(AXES, None, None, None))
    return jax.shard_map(local, mesh=mesh, in_specs=in_specs, out_specs=out_specs, check_vma=False)
```

time: 128 us -> 124 us (0.969)
  Pallas kernels: 59.4 us -> 49 us
  waiting for transfers between devices: 0.03 us -> 9.73 us
  local copies, waits for them, and re-layouts: 10.2 us -> 3.97 us
  other arithmetic: 15.5 us -> 20 us
    ppermute x12, waiting for transfers between devices: 0.03 us -> 9.73 us  [shifted(): return lax.ppermute(x, AXES, [((i - distance) % n, i) for i in range(n)])]
    slice x2 -> x0, local copies, waits for them, and re-layouts: 6.2 us -> none  [the longest x1 3.12 us: local(): a2 = shifted(density[:HALF].reshape(PIECE, BS, BS), -1)]
    pallas_call x1, Pallas kernels: 20.4 us -> 15.7 us  [near_step(): pl.pallas_call(near_kernel, out_shape=(f32(4 * KS), f32(8 * KS), f32(4 *...]
    pallas_call x1, Pallas kernels: 15.9 us -> 12.7 us  [pair_lists(): pl.pallas_call(list_kernel, out_shape=(jax.ShapeDtypeStruct((LIST_OFF[-1]...]
    pallas_call x2 -> x3, Pallas kernels: 23.1 us -> 20.6 us  [the longest x2 19 us: far_step(): pl.pallas_call(functools.partial(far_kernel, final), out_shape=f32(4 * KC...]
    reduce_or x1 -> x2, other arithmetic: 0.08 us -> 1.73 us  [the longest x1 1.65 us: pair_tables(): in_cube = jnp.any(sq12[None, :, :, None] == cu4[:, None, None, :], axis=-1)]
  transfers between devices with their start and end apart: 12 -> 12, of which waited for: 0 -> 3; matrix products, arithmetic and copies ran while one was open for 19% -> 18% of each run, Pallas kernels for 39% -> 33%
where the time goes in v3:
time: 124 us
  Pallas kernels  49 us (40%)
  starting transfers between devices  39.5 us (32%)
  other arithmetic  20 us (16%)
  waiting for transfers between devices  9.73 us (8%)
  local copies, waits for them, and re-layouts  3.97 us (3%)
  between operations  1.28 us (1%)
    ppermute x12, starting transfers between devices, shifted(): return lax.ppermute(x, AXES, [((i - distance) % n, i) for i in range(n)])  39.5 us
    pallas_call x2, Pallas kernels, far_step(): pl.pallas_call(functools.partial(far_kernel, final), out_shape=f32(4 * KC...  19 us
    pallas_call x1, Pallas kernels, near_step(): pl.pallas_call(near_kernel, out_shape=(f32(4 * KS), f32(8 * KS), f32(4 *...  15.7 us
    pallas_call x1, Pallas kernels, pair_lists(): pl.pallas_call(list_kernel, out_shape=(jax.ShapeDtypeStruct((LIST_OFF[-1]...  12.7 us
    ppermute x12, waiting for transfers between devices, shifted(): return lax.ppermute(x, AXES, [((i - distance) % n, i) for i in range(n)])  9.73 us
    reduce_sum x6, other arithmetic, pick(): return jnp.sum(jnp.where(hot.reshape(shape), table, 0), axis=index.ndim)  5.66 us
    or x8, other arithmetic, entries(): left[:, None, :] | right << 8 | target[:, :, None] << 16  3.09 us
  transfers between devices with their start and end apart: 12, of which 3 were waited for; matrix products, arithmetic and copies ran while one was open for 18% of the time, Pallas kernels for 33%

profile of v3, /device:TPU:0, one launch (start us, length us, event | category | flops | bytes accessed | tf_op | source)
XLA Modules:
  0.0 123.5 jit_solution(9495645453358824918)
XLA Ops:
  0.6 0.8 pad_add_fusion.4
  1.4 8.4 %collective-permute-start.3 = (s32[4,24]{1,0:T(4,128)S(1)}, s32[4,24]{1,0:T(4,128)S(1)}, u32[]{:S(2)}, u32[]{:S(2)}) collective-permute-start(s32[4,24]{1,0:T(4,128)S(1)} %pad_add_fusion.4), channel_id=1, source_target_pairs={{2,0},{3,1},{4,2},{5,3},{6,4},{7,5},{8,6},{9,7},{10,8},{11,9},{12,... | collective-permute-start | bytes 1160 | tf_op jit(solution)/shard_map/ppermute | solution.py:29
  9.8 0.8 collective-permute-start.2
  10.6 1.3 %collective-permute-start.1 = (s32[4,24]{1,0:T(4,128)S(1)}, s32[4,24]{1,0:T(4,128)S(1)}, u32[]{:S(2)}, u32[]{:S(2)}) collective-permute-start(s32[4,24]{1,0:T(4,128)S(1)} %pad_add_fusion.4), channel_id=1, source_target_pairs={{255,0},{0,1},{1,2},{2,3},{3,4},{4,5},{5,6},{6,7},{7,8},{8,9},{9,1... | collective-permute-start | bytes 1160 | tf_op jit(solution)/shard_map/ppermute | solution.py:29
  12.5 1.6 %split.1 = (f32[16,128,128]{2,1,0:T(8,128)S(1)}, f32[16,128,128]{2,1,0:T(8,128)S(1)}) custom-call(f32[32,128,128]{2,1,0:T(8,128)} %bitcast.28), custom_call_target="tpu_custom_call" | custom-call | bytes 4000000 | tf_op jit(solution)/shard_map/split/pallas_call | solution.py:351
  14.1 6.6 %collective-permute-start.7 = (f32[16,128,128]{2,1,0:T(8,128)S(1)}, f32[16,128,128]{2,1,0:T(8,128)S(1)}, u32[]{:S(2)}, u32[]{:S(2)}) collective-permute-start(f32[16,128,128]{2,1,0:T(8,128)S(1)} %get-tuple-element.33), channel_id=1, source_target_pairs={{1,0},{2,1},{3,2},{4,3},{5,4},{6,5},{7,6},{8,7},{9,8},{10,9},{11,1... | collective-permute-start | bytes 3145736 | tf_op jit(solution)/shard_map/ppermute | solution.py:29
  22.3 1.0 fusion.7
  23.4 0.8 pad_add_fusion.5
  24.2 0.8 pad_add_fusion.2
  25.2 0.9 select_reduce_fusion.9
  26.1 0.9 select_reduce_fusion.8
  27.1 1.0 select_reduce_fusion.6
  28.9 0.8 select_reduce_fusion.7
  30.2 1.7 %compare_reduce_fusion = pred[4,12,16]{2,1,0:T(8,128)(4,1)S(1)} fusion(s32[4,24]{1,0:T(4,128)} %param.26, s32[12,16]{1,0:T(8,128)S(1)} %slice.121), kind=kLoop, calls=%fused_computation.2 | loop fusion | flops 36096 | bytes 1920 | tf_op jit(solution)/shard_map/reduce_or | solution.py:71
  32.0 0.9 select_reduce_fusion.2
  33.3 0.8 shift-left_or_fusion.2
  35.2 1.7 %select_reduce_fusion.1 = s32[12,8,8]{2,1,0:T(8,128)S(1)} fusion(s32[20,8]{0,1:T(8,128)S(1)} %copy.56, pred[12,8,20]{2,1,0:T(8,128)(4,1)S(1)} %iota_compare_fusion.2), kind=kLoop, calls=%fused_computation.1 | loop fusion | flops 29952 | bytes 5632 | tf_op jit(solution)/shard_map/reduce_sum | solution.py:50
  37.9 0.8 shift-left_or_fusion.3
  38.7 0.8 shift-left_or_fusion.1
  39.6 0.8 shift-left_or_fusion
  41.0 6.8 %collective-permute-start.5 = (f32[16,128,128]{2,1,0:T(8,128)S(1)}, f32[16,128,128]{2,1,0:T(8,128)}, u32[]{:S(2)}, u32[]{:S(2)}) collective-permute-start(f32[16,128,128]{2,1,0:T(8,128)S(1)} %get-tuple-element.34), channel_id=1, source_target_pairs={{1,0},{2,1},{3,2},{4,3},{5,4},{6,5},{7,6},{8,7},{9,8},{10,9},{11,1... | collective-permute-start | bytes 3145736 | tf_op jit(solution)/shard_map/ppermute | solution.py:29
  48.5 0.8 select_reduce_fusion.4
  49.6 0.8 reshape.321.table
  50.4 0.9 collective-permute-done.6.a1
  51.3 7.2 %collective-permute-start.11 = (f32[16,128,128]{2,1,0:T(8,128)S(1)}, f32[16,128,128]{2,1,0:T(8,128)}, u32[]{:S(2)}, u32[]{:S(2)}) collective-permute-start(f32[16,128,128]{2,1,0:T(8,128)S(1)} %collective-permute-done.7.a2), channel_id=1, source_target_pairs={{1,0},{2,1},{3,2},{4,3},{5,4},{6,5},{7,6},{8,7},{9,8},{10,9},{11,1... | collective-permute-start | bytes 3145736 | tf_op jit(solution)/shard_map/ppermute | solution.py:29
  58.5 12.7 %pair_lists.1 = (s32[5472]{0:T(1024)}, s32[6]{0:T(128)}) custom-call(s32[5376]{0:T(1024)} %reshape.321.table, s32[672]{0:T(1024)} %get-tuple-element.43.hits), custom_call_target="tpu_custom_call" | custom-call | flops 20000000 | bytes 40000000 | tf_op jit(solution)/shard_map/pair_lists/pallas_call | solution.py:132
  71.2 2.6 %collective-permute-done.4.b1 = f32[16,128,128]{2,1,0:T(8,128)} collective-permute-done((f32[16,128,128]{2,1,0:T(8,128)S(1)}, f32[16,128,128]{2,1,0:T(8,128)}, u32[]{:S(2)}, u32[]{:S(2)}) %collective-permute-start.4) | collective-permute-done | bytes 1048608 | tf_op jit(solution)/shard_map/ppermute | solution.py:29
  73.8 7.2 %collective-permute-start.9 = (f32[16,128,128]{2,1,0:T(8,128)}, f32[16,128,128]{2,1,0:T(8,128)S(1)}, u32[]{:S(2)}, u32[]{:S(2)}) collective-permute-start(f32[16,128,128]{2,1,0:T(8,128)} %collective-permute-done.5.b2), channel_id=1, source_target_pairs={{1,0},{2,1},{3,2},{4,3},{5,4},{6,5},{7,6},{8,7},{9,8},{10,9},{11,1... | collective-permute-start | bytes 3145736 | tf_op jit(solution)/shard_map/ppermute | solution.py:29
  82.3 15.7 %near_step.1 = (f32[64,128,128]{2,1,0:T(8,128)}, f32[128,128,128]{2,1,0:T(8,128)}, f32[96,128,128]{2,1,0:T(8,128)}, bf16[97,128,256]{2,1,0:T(8,128)(2,1)}) custom-call(s32[5472]{0:T(1024)S(1)} %copy-done, s32[6]{0:T(128)S(1)} %copy-done.2, s32[96]{0:T(128)S(1)} %select_n.145.carry, f32[16,128,128]{2,1,0:T(8,128)} %collective-permute-done.4.b1, ...), custom_call_target="tpu_custom_call" | custom-call | flops 20000000000 | bytes 60000000 | tf_op jit(solution)/shard_map/near_step/pallas_call | solution.py:295
  98.1 11.1 %middle_step.1 = (f32[64,128,128]{2,1,0:T(8,128)S(1)}, f32[96,128,128]{2,1,0:T(8,128)S(1)}) custom-call(s32[5472]{0:T(1024)S(1)} %copy-done.1, s32[6]{0:T(128)S(1)} %copy-done.3, f32[16,128,128]{2,1,0:T(8,128)} %collective-permute-done.10.below, f32[16,128,128]{2,1,0:T(8,128)} %collective-permute-done.11.above, ...), custom_call_target="tpu_custom_call" | custom-call | flops 10000000000 | bytes 40000000 | tf_op jit(solution)/shard_map/middle_step/pallas_call | solution.py:320
  109.2 6.2 %collective-permute-done.8.below = f32[16,128,128]{2,1,0:T(8,128)S(1)} collective-permute-done((f32[16,128,128]{2,1,0:T(8,128)}, f32[16,128,128]{2,1,0:T(8,128)S(1)}, u32[]{:S(2)}, u32[]{:S(2)}) %collective-permute-start.8) | collective-permute-done | bytes 1048608 | tf_op jit(solution)/shard_map/ppermute | solution.py:29
  115.4 8.0 %last_step.1 = f32[96,128,128]{2,1,0:T(8,128)} custom-call(s32[5472]{0:T(1024)S(1)} %copy-done.1, s32[6]{0:T(128)S(1)} %copy-done.3, f32[16,128,128]{2,1,0:T(8,128)S(1)} %collective-permute-done.8.below, f32[16,128,128]{2,1,0:T(8,128)S(1)} %collective-permute-done.9.above, bf16[97,128,256]{2,1,0:T(8,128)(2,1)} %get-tuple-element.55.left_in, ...), custom_call_target="tpu_custom_call" | custom-call | flops 10000000000 | bytes 40000000 | tf_op jit(solution)/shard_map/last_step/pallas_call | solution.py:320
  (103 shorter events, 9.4 us)
Async XLA Ops:
  1.4 19.4 %collective-permute-start.3 = (s32[4,24]{1,0:T(4,128)S(1)}, s32[4,24]{1,0:T(4,128)S(1)}, u32[]{:S(2)}, u32[]{:S(2)}) collective-permute-start(s32[4,24]{1,0:T(4,128)S(1)} %pad_add_fusion.4), channel_id=1, source_target_pairs={{2,0},{3,1},{4,2},{5,3},{6,4},{7,5},{8,6},{9,7},{10,8},{11,9},{12,... | collective-permute-start | bytes 1160 | tf_op jit(solution)/shard_map/ppermute | solution.py:29
  9.8 11.1 %collective-permute-start.2 = (s32[4,24]{1,0:T(4,128)S(1)}, s32[4,24]{1,0:T(4,128)S(1)}, u32[]{:S(2)}, u32[]{:S(2)}) collective-permute-start(s32[4,24]{1,0:T(4,128)S(1)} %pad_add_fusion.4), channel_id=1, source_target_pairs={{1,0},{2,1},{3,2},{4,3},{5,4},{6,5},{7,6},{8,7},{9,8},{10,9},{11,1... | collective-permute-start | bytes 1160 | tf_op jit(solution)/shard_map/ppermute | solution.py:29
  10.6 10.4 %collective-permute-start.1 = (s32[4,24]{1,0:T(4,128)S(1)}, s32[4,24]{1,0:T(4,128)S(1)}, u32[]{:S(2)}, u32[]{:S(2)}) collective-permute-start(s32[4,24]{1,0:T(4,128)S(1)} %pad_add_fusion.4), channel_id=1, source_target_pairs={{255,0},{0,1},{1,2},{2,3},{3,4},{4,5},{5,6},{6,7},{7,8},{8,9},{9,1... | collective-permute-start | bytes 1160 | tf_op jit(solution)/shard_map/ppermute | solution.py:29
  11.8 9.1 %collective-permute-start = (s32[4,24]{1,0:T(4,128)S(1)}, s32[4,24]{1,0:T(4,128)S(1)}, u32[]{:S(2)}, u32[]{:S(2)}) collective-permute-start(s32[4,24]{1,0:T(4,128)S(1)} %pad_add_fusion.4), channel_id=1, source_target_pairs={{254,0},{255,1},{0,2},{1,3},{2,4},{3,5},{4,6},{5,7},{6,8},{7,9},{8... | collective-permute-start | bytes 1160 | tf_op jit(solution)/shard_map/ppermute | solution.py:29
  14.1 36.3 %collective-permute-start.7 = (f32[16,128,128]{2,1,0:T(8,128)S(1)}, f32[16,128,128]{2,1,0:T(8,128)S(1)}, u32[]{:S(2)}, u32[]{:S(2)}) collective-permute-start(f32[16,128,128]{2,1,0:T(8,128)S(1)} %get-tuple-element.33), channel_id=1, source_target_pairs={{1,0},{2,1},{3,2},{4,3},{5,4},{6,5},{7,6},{8,7},{9,8},{10,9},{11,1... | collective-permute-start | bytes 3145736 | tf_op jit(solution)/shard_map/ppermute | solution.py:29
  20.8 30.5 %collective-permute-start.6 = (f32[16,128,128]{2,1,0:T(8,128)S(1)}, f32[16,128,128]{2,1,0:T(8,128)}, u32[]{:S(2)}, u32[]{:S(2)}) collective-permute-start(f32[16,128,128]{2,1,0:T(8,128)S(1)} %get-tuple-element.34), channel_id=1, source_target_pairs={{255,0},{0,1},{1,2},{2,3},{3,4},{4,5},{5,6},{6,7},{7,8},{8,9},{9,1... | collective-permute-start | bytes 3145736 | tf_op jit(solution)/shard_map/ppermute | solution.py:29
  40.5 33.3 %collective-permute-start.4 = (f32[16,128,128]{2,1,0:T(8,128)S(1)}, f32[16,128,128]{2,1,0:T(8,128)}, u32[]{:S(2)}, u32[]{:S(2)}) collective-permute-start(f32[16,128,128]{2,1,0:T(8,128)S(1)} %get-tuple-element.33), channel_id=1, source_target_pairs={{255,0},{0,1},{1,2},{2,3},{3,4},{4,5},{5,6},{6,7},{7,8},{8,9},{9,1... | collective-permute-start | bytes 3145736 | tf_op jit(solution)/shard_map/ppermute | solution.py:29
  41.0 32.8 %collective-permute-start.5 = (f32[16,128,128]{2,1,0:T(8,128)S(1)}, f32[16,128,128]{2,1,0:T(8,128)}, u32[]{:S(2)}, u32[]{:S(2)}) collective-permute-start(f32[16,128,128]{2,1,0:T(8,128)S(1)} %get-tuple-element.34), channel_id=1, source_target_pairs={{1,0},{2,1},{3,2},{4,3},{5,4},{6,5},{7,6},{8,7},{9,8},{10,9},{11,1... | collective-permute-start | bytes 3145736 | tf_op jit(solution)/shard_map/ppermute | solution.py:29
  51.3 46.7 %collective-permute-start.10 = (f32[16,128,128]{2,1,0:T(8,128)}, f32[16,128,128]{2,1,0:T(8,128)}, u32[]{:S(2)}, u32[]{:S(2)}) collective-permute-start(f32[16,128,128]{2,1,0:T(8,128)} %collective-permute-done.6.a1), channel_id=1, source_target_pairs={{255,0},{0,1},{1,2},{2,3},{3,4},{4,5},{5,6},{6,7},{7,8},{8,9},{9,1... | collective-permute-start | bytes 3145736 | tf_op jit(solution)/shard_map/ppermute | solution.py:29
  51.3 46.7 %collective-permute-start.11 = (f32[16,128,128]{2,1,0:T(8,128)S(1)}, f32[16,128,128]{2,1,0:T(8,128)}, u32[]{:S(2)}, u32[]{:S(2)}) collective-permute-start(f32[16,128,128]{2,1,0:T(8,128)S(1)} %collective-permute-done.7.a2), channel_id=1, source_target_pairs={{1,0},{2,1},{3,2},{4,3},{5,4},{6,5},{7,6},{8,7},{9,8},{10,9},{11,1... | collective-permute-start | bytes 3145736 | tf_op jit(solution)/shard_map/ppermute | solution.py:29
  73.8 24.3 %copy-start.3 = (s32[6]{0:T(128)S(1)}, s32[6]{0:T(128)}, u32[]{:S(2)}) copy-start(s32[6]{0:T(128)} %get-tuple-element.48.counts) | copy-start | bytes 76
  73.8 41.6 %collective-permute-start.8 = (f32[16,128,128]{2,1,0:T(8,128)}, f32[16,128,128]{2,1,0:T(8,128)S(1)}, u32[]{:S(2)}, u32[]{:S(2)}) collective-permute-start(f32[16,128,128]{2,1,0:T(8,128)} %collective-permute-done.4.b1), channel_id=1, source_target_pairs={{255,0},{0,1},{1,2},{2,3},{3,4},{4,5},{5,6},{6,7},{7,8},{8,9},{9,1... | collective-permute-start | bytes 3145736 | tf_op jit(solution)/shard_map/ppermute | solution.py:29
  73.8 41.6 %collective-permute-start.9 = (f32[16,128,128]{2,1,0:T(8,128)}, f32[16,128,128]{2,1,0:T(8,128)S(1)}, u32[]{:S(2)}, u32[]{:S(2)}) collective-permute-start(f32[16,128,128]{2,1,0:T(8,128)} %collective-permute-done.5.b2), channel_id=1, source_target_pairs={{1,0},{2,1},{3,2},{4,3},{5,4},{6,5},{7,6},{8,7},{9,8},{10,9},{11,1... | collective-permute-start | bytes 3145736 | tf_op jit(solution)/shard_map/ppermute | solution.py:29
  81.0 0.7 copy-start
  81.7 0.6 copy-start.2
  82.3 15.8 %copy-start.1 = (s32[5472]{0:T(1024)S(1)}, s32[5472]{0:T(1024)}, u32[]{:S(2)}) copy-start(s32[5472]{0:T(1024)} %get-tuple-element.47.lists) | copy-start | bytes 65668

commit v4 on v3

--- a/solution.py
+++ b/solution.py
@@ -10,8 +10,10 @@
 
 AXES = ("row", "col")
 ROWS, KP, KS, KC, BS = 4, 8, 16, 24, 128
-HALF = ROWS // 2
-PIECE = HALF * KP
+BLOCKS = ROWS * KP
+PIECE = BLOCKS // 2
+FIRST = PIECE + 4
+SECOND = BLOCKS - FIRST
 GROUP = 16
 ZERO_LEFT = 12 * KP
 
@@ -188,9 +190,14 @@
 def near_kernel(lists, counts, carry, b1, a1, own, a2, b2, s_out, sp_out, c_out, cut_out, stage, cut, total, s_cut, c, sems):
     loads = []
     for i, (src, at, n) in enumerate(
-        ((own, 2, 2), (a1, 1, 1), (a2, 4, 1), (b1, 0, 1), (b2, 5, 1))
+        (
+            (own, BLOCKS, BLOCKS),
+            (a1, SECOND, FIRST),
+            (a2, 2 * BLOCKS, FIRST),
+            (b1, 0, SECOND),
+            (b2, 2 * BLOCKS + FIRST, SECOND),
+        )
     ):
-        at, n = at * PIECE, n * PIECE
         loads.append((pltpu.make_async_copy(src, stage.at[pl.ds(at, n)], sems.at[i]), at, n))
     for copy, _, _ in loads:
         copy.start()
@@ -228,14 +235,23 @@
 
 def far_kernel(final, lists, counts, below, above, left_in, sp_in, c_in, *refs):
     if final:
-        out, stage, left, right, sp, s_cut, c, sems = refs
+        more_below, more_above, out, stage, left, right, sp, s_cut, c, sems = refs
     else:
         sp_out, out, stage, left, right, sp, s_cut, c, sems = refs
     which = 4 if final else 2
-    loads = [
-        pltpu.make_async_copy(below, stage.at[pl.ds(0, PIECE)], sems.at[0]),
-        pltpu.make_async_copy(above, stage.at[pl.ds(PIECE, PIECE)], sems.at[1]),
-    ]
+    extra = FIRST - PIECE
+    if final:
+        pieces = (
+            (below, 0, 0, SECOND),
+            (more_below, 0, SECOND, extra),
+            (more_above, PIECE, PIECE, extra),
+            (above, 0, PIECE + extra, SECOND),
+        )
+    else:
+        pieces = ((below, extra, 0, PIECE), (above, 0, PIECE, PIECE))
+    loads = []
+    for i, (src, at, to, n) in enumerate(pieces):
+        loads.append(pltpu.make_async_copy(src.at[pl.ds(at, n)], stage.at[pl.ds(to, n)], sems.at[12 + i]))
     ranges = ((0, 2 * KP), (10 * KP, 2 * KP + 1)) if final else ((0, 4 * KP), (8 * KP, 4 * KP + 1))
     for i, (at, n) in enumerate(ranges + ((4 * KP, 4 * KP),)):
         loads.append(pltpu.make_async_copy(left_in.at[pl.ds(at, n)], left.at[pl.ds(at, n)], sems.at[2 + i]))
@@ -246,10 +262,10 @@
         copy.start()
     zero(right, 2 * PIECE)
     zero(s_cut, 4 * KS)
-    for i, copy in enumerate(loads[:2]):
-        copy.wait()
-        each(i * PIECE, (i + 1) * PIECE, lambda q: put(right, q, stage[q]))
-    for copy in loads[2:]:
+    for copy, (_, _, to, n) in zip(loads, pieces):
+        copy.wait()
+        each(to, to + n, lambda q: put(right, q, stage[q]))
+    for copy in loads[len(pieces) :]:
         copy.wait()
     multiply(which, lists, counts, left, right, sp)
     done = []
@@ -276,7 +292,6 @@
 
 SMEM = pl.BlockSpec(memory_space=pltpu.SMEM)
 ANY = pl.BlockSpec(memory_space=pl.ANY)
-VMEM = pl.BlockSpec(memory_space=pltpu.VMEM)
 
 
 def f32(n):
@@ -311,16 +326,16 @@
             pltpu.SemaphoreType.DMA((9,)),
         ],
         compiler_params=pltpu.CompilerParams(vmem_limit_bytes=48 * 1024 * 1024),
-        cost_estimate=pl.CostEstimate(flops=20_000_000_000, bytes_accessed=60_000_000, transcendentals=0),
+        cost_estimate=pl.CostEstimate(flops=10_000_000_000, bytes_accessed=30_000_000, transcendentals=0),
         name="near_step",
     )(lists, counts, carry, *pieces)
 
 
-def far_step(final, lists, counts, below, above, left, sp, c):
+def far_step(final, lists, counts, below, above, left, sp, c, *more):
     return pl.pallas_call(
         functools.partial(far_kernel, final),
         out_shape=f32(4 * KC) if final else (f32(4 * KS), f32(4 * KC)),
-        in_specs=[SMEM] * 2 + [ANY] * 5,
+        in_specs=[SMEM] * 2 + [ANY] * (5 + len(more)),
         out_specs=ANY if final else (ANY, ANY),
         scratch_shapes=[
             vmem_f32(2 * PIECE),
@@ -329,31 +344,39 @@
             vmem_f32((4 if final else 8) * KS),
             vmem_cut(4 * KS),
             vmem_f32(4 * KC),
-            pltpu.SemaphoreType.DMA((12,)),
+            pltpu.SemaphoreType.DMA((16,)),
         ],
         compiler_params=pltpu.CompilerParams(vmem_limit_bytes=36 * 1024 * 1024),
         cost_estimate=pl.CostEstimate(flops=10_000_000_000, bytes_accessed=40_000_000, transcendentals=0),
         name="last_step" if final else "middle_step",
-    )(lists, counts, below, above, left, sp, c)
-
-
-def split_kernel(src, one, two, sems):
-    copies = [
-        pltpu.make_async_copy(src.at[pl.ds(i * PIECE, PIECE)], dst, sems.at[i]) for i, dst in enumerate((one, two))
-    ]
-    for copy in copies:
+    )(lists, counts, below, above, left, sp, c, *more)
+
+
+def split_kernel(ranges, src, one, two, stage, sems):
+    loads, stores, to = [], [], 0
+    for i, ((at, n), dst) in enumerate(zip(ranges, (one, two))):
+        for q in range(2):
+            half = n // 2
+            piece, k = stage.at[pl.ds(to, half)], 2 * i + q
+            loads.append(pltpu.make_async_copy(src.at[pl.ds(at + q * half, half)], piece, sems.at[k]))
+            stores.append(pltpu.make_async_copy(piece, dst.at[pl.ds(q * half, half)], sems.at[4 + k]))
+            to += half
+    for copy in loads:
         copy.start()
-    for copy in copies:
-        copy.wait()
-
-
-def split(blocks):
+    for load, store in zip(loads, stores):
+        load.wait()
+        store.start()
+    for copy in stores:
+        copy.wait()
+
+
+def split(blocks, *ranges):
     return pl.pallas_call(
-        split_kernel,
-        out_shape=(vmem_f32(PIECE), vmem_f32(PIECE)),
+        functools.partial(split_kernel, ranges),
+        out_shape=tuple(f32(n) for _, n in ranges),
         in_specs=[ANY],
-        out_specs=(VMEM, VMEM),
-        scratch_shapes=[pltpu.SemaphoreType.DMA((2,))],
+        out_specs=(ANY, ANY),
+        scratch_shapes=[vmem_f32(sum(n for _, n in ranges)), pltpu.SemaphoreType.DMA((8,))],
         cost_estimate=pl.CostEstimate(flops=0, bytes_accessed=4_000_000, transcendentals=0),
         name="split",
     )(blocks)
@@ -367,13 +390,14 @@
 
     cols = jnp.concatenate([pattern, square_target], axis=1)
     cols_from = [shifted(cols, d) for d in (2, 1, -1, -2)]
-    own = density.reshape(2 * PIECE, BS, BS)
-    lower, upper = split(own)
-    a1, a2 = shifted(upper, 1), shifted(lower, -1)
-    lower, upper, pattern, square_target, cube_target, *cols_from = hold(
-        (lower, upper, pattern, square_target, cube_target, *cols_from)
+    own = density.reshape(BLOCKS, BS, BS)
+    send_up, send_down = split(own, (SECOND, FIRST), (0, FIRST))
+    a1, a2 = shifted(send_up, 1), shifted(send_down, -1)
+    rest, pattern, square_target, cube_target, *cols_from = hold(
+        (own, pattern, square_target, cube_target, *cols_from)
     )
-    b1, b2 = shifted(lower, 1), shifted(upper, -1)
+    send_up, send_down = split(rest, (0, SECOND), (FIRST, SECOND))
+    b1, b2 = shifted(send_up, 1), shifted(send_down, -1)
     near = jnp.concatenate(cols_from[:2] + [jnp.concatenate([pattern, square_target], axis=1)] + cols_from[2:], axis=0)
     table, hits, carry = pair_tables(base, near[:, :KP], near[4:16, KP:], cube_target, total_rows)
     a1, a2, table, hits, carry = hold((a1, a2, table, hits, carry))
@@ -384,7 +408,7 @@
 
     s_own, sp, c, left = near_step(lists, counts, carry, (b1, a1, own, a2, b2))
     sp, c = far_step(False, lists, counts, c1, c2, left, sp, c)
-    out = far_step(True, lists, counts, d1, d2, left, sp, c)
+    out = far_step(True, lists, counts, d1, d2, left, sp, c, c1, c2)
     return s_own.reshape(ROWS, KS, BS, BS), out.reshape(ROWS, KC, BS, BS)
 
 

time: 124 us -> 121 us (0.976)
  waiting for transfers between devices: 9.73 us -> 0.52 us
  Pallas kernels: 49 us -> 52.5 us
  local copies, waits for them, and re-layouts: 3.97 us -> 5.74 us
    ppermute x12, waiting for transfers between devices: 9.73 us -> 0.52 us  [shifted(): return lax.ppermute(x, AXES, [((i - distance) % n, i) for i in range(n)])]
    pallas_call x1 -> x2, Pallas kernels: 1.56 us -> 4.86 us  [split(): pl.pallas_call(functools.partial(split_kernel, ranges), out_shape=tuple((...]
  transfers between devices with their start and end apart: 12 -> 12, of which waited for: 3 -> 1; matrix products, arithmetic and copies ran while one was open for 18% -> 19% of each run, Pallas kernels for 33% -> 38%
where the time goes in v4:
time: 121 us; the launch traced here: 119 us
  Pallas kernels  52.5 us (43%)
  starting transfers between devices  40.1 us (33%)
  other arithmetic  19.3 us (16%)
  local copies, waits for them, and re-layouts  5.74 us (5%)
  between operations  1.33 us (1%)
    ppermute x12, starting transfers between devices, shifted(): return lax.ppermute(x, AXES, [((i - distance) % n, i) for i in range(n)])  40.1 us
    pallas_call x2, Pallas kernels, far_step(): pl.pallas_call(functools.partial(far_kernel, final), out_shape=f32(4 * KC...  18.7 us
    pallas_call x1, Pallas kernels, near_step(): pl.pallas_call(near_kernel, out_shape=(f32(4 * KS), f32(8 * KS), f32(4 *...  16.2 us
    pallas_call x1, Pallas kernels, pair_lists(): pl.pallas_call(list_kernel, out_shape=(jax.ShapeDtypeStruct((LIST_OFF[-1]...  12.7 us
    reduce_sum x6, other arithmetic, pick(): return jnp.sum(jnp.where(hot.reshape(shape), table, 0), axis=index.ndim)  5.66 us
    pallas_call x2, Pallas kernels, split(): pl.pallas_call(functools.partial(split_kernel, ranges), out_shape=tuple((...  4.86 us
    or x8, other arithmetic, entries(): left[:, None, :] | right << 8 | target[:, :, None] << 16  3.09 us
  transfers between devices with their start and end apart: 12, of which 1 were waited for; matrix products, arithmetic and copies ran while one was open for 19% of the time, Pallas kernels for 38%

profile of v4, /device:TPU:0, one launch (start us, length us, event | category | flops | bytes accessed | tf_op | source)
XLA Modules:
  0.0 119.5 jit_solution(11113888224758176443)
XLA Ops:
  0.6 0.8 pad_add_fusion.4
  1.4 8.4 %collective-permute-start.3 = (s32[4,24]{1,0:T(4,128)S(1)}, s32[4,24]{1,0:T(4,128)S(1)}, u32[]{:S(2)}, u32[]{:S(2)}) collective-permute-start(s32[4,24]{1,0:T(4,128)S(1)} %pad_add_fusion.4), channel_id=1, source_target_pairs={{2,0},{3,1},{4,2},{5,3},{6,4},{7,5},{8,6},{9,7},{10,8},{11,9},{12,... | collective-permute-start | bytes 1160 | tf_op jit(solution)/shard_map/ppermute | solution.py:31
  9.8 0.8 collective-permute-start.2
  10.6 1.3 %collective-permute-start.1 = (s32[4,24]{1,0:T(4,128)S(1)}, s32[4,24]{1,0:T(4,128)S(1)}, u32[]{:S(2)}, u32[]{:S(2)}) collective-permute-start(s32[4,24]{1,0:T(4,128)S(1)} %pad_add_fusion.4), channel_id=1, source_target_pairs={{255,0},{0,1},{1,2},{2,3},{3,4},{4,5},{5,6},{6,7},{7,8},{8,9},{9,1... | collective-permute-start | bytes 1160 | tf_op jit(solution)/shard_map/ppermute | solution.py:31
  12.6 2.6 %split.3 = (f32[20,128,128]{2,1,0:T(8,128)}, f32[20,128,128]{2,1,0:T(8,128)}) custom-call(f32[32,128,128]{2,1,0:T(8,128)} %bitcast.28), custom_call_target="tpu_custom_call" | custom-call | bytes 4000000 | tf_op jit(solution)/shard_map/split/pallas_call | solution.py:374
  15.4 7.2 %collective-permute-start.7 = (f32[20,128,128]{2,1,0:T(8,128)}, f32[20,128,128]{2,1,0:T(8,128)S(1)}, u32[]{:S(2)}, u32[]{:S(2)}) collective-permute-start(f32[20,128,128]{2,1,0:T(8,128)} %get-tuple-element.36), channel_id=1, source_target_pairs={{1,0},{2,1},{3,2},{4,3},{5,4},{6,5},{7,6},{8,7},{9,8},{10,9},{11,1... | collective-permute-start | bytes 3932168 | tf_op jit(solution)/shard_map/ppermute | solution.py:31
  24.0 1.0 fusion.7
  25.1 0.8 pad_add_fusion.5
  25.9 0.8 pad_add_fusion.2
  26.8 0.9 select_reduce_fusion.9
  27.7 0.9 select_reduce_fusion.8
  28.8 1.0 select_reduce_fusion.6
  30.6 0.8 select_reduce_fusion.7
  31.8 1.7 %compare_reduce_fusion = pred[4,12,16]{2,1,0:T(8,128)(4,1)S(1)} fusion(s32[4,24]{1,0:T(4,128)} %param.26, s32[12,16]{1,0:T(8,128)S(1)} %slice.121), kind=kLoop, calls=%fused_computation.2 | loop fusion | flops 36096 | bytes 1920 | tf_op jit(solution)/shard_map/reduce_or | solution.py:73
  33.6 0.9 select_reduce_fusion.2
  35.0 0.8 shift-left_or_fusion.2
  36.1 0.7 broadcast_or_fusion
  36.9 1.7 %select_reduce_fusion.1 = s32[12,8,8]{2,1,0:T(8,128)S(1)} fusion(s32[20,8]{0,1:T(8,128)S(1)} %copy.56, pred[12,8,20]{2,1,0:T(8,128)(4,1)S(1)} %iota_compare_fusion.2), kind=kLoop, calls=%fused_computation.1 | loop fusion | flops 29952 | bytes 5632 | tf_op jit(solution)/shard_map/reduce_sum | solution.py:52
  39.5 0.8 shift-left_or_fusion.3
  40.4 0.8 shift-left_or_fusion.1
  41.3 0.8 shift-left_or_fusion
  42.2 2.2 %split.2 = (f32[12,128,128]{2,1,0:T(8,128)}, f32[12,128,128]{2,1,0:T(8,128)}) custom-call(f32[32,128,128]{2,1,0:T(8,128)} %bitcast.29), custom_call_target="tpu_custom_call" | custom-call | bytes 4000000 | tf_op jit(solution)/shard_map/split/pallas_call | solution.py:374
  44.5 7.2 %collective-permute-start.5 = (f32[12,128,128]{2,1,0:T(8,128)}, f32[12,128,128]{2,1,0:T(8,128)}, u32[]{:S(2)}, u32[]{:S(2)}) collective-permute-start(f32[12,128,128]{2,1,0:T(8,128)} %get-tuple-element.34), channel_id=1, source_target_pairs={{1,0},{2,1},{3,2},{4,3},{5,4},{6,5},{7,6},{8,7},{9,8},{10,9},{11,1... | collective-permute-start | bytes 2359304 | tf_op jit(solution)/shard_map/ppermute | solution.py:31
  52.6 0.9 copy.70
  53.5 1.8 %reshape.321.table = s32[5376]{0:T(1024)} reshape(s32[672,8]{1,0:T(8,128)} %copy.70) | data formatting | bytes 43008 | tf_op jit(solution)/shard_map/reshape | solution.py:98
  55.3 7.2 %collective-permute-start.11 = (f32[20,128,128]{2,1,0:T(8,128)S(1)}, f32[20,128,128]{2,1,0:T(8,128)}, u32[]{:S(2)}, u32[]{:S(2)}) collective-permute-start(f32[20,128,128]{2,1,0:T(8,128)S(1)} %collective-permute-done.7.a2), channel_id=1, source_target_pairs={{1,0},{2,1},{3,2},{4,3},{5,4},{6,5},{7,6},{8,7},{9,8},{10,9},{11,1... | collective-permute-start | bytes 3932168 | tf_op jit(solution)/shard_map/ppermute | solution.py:31
  62.5 12.7 %pair_lists.1 = (s32[5472]{0:T(1024)}, s32[6]{0:T(128)}) custom-call(s32[5376]{0:T(1024)} %reshape.321.table, s32[672]{0:T(1024)} %get-tuple-element.45.hits), custom_call_target="tpu_custom_call" | custom-call | flops 20000000 | bytes 40000000 | tf_op jit(solution)/shard_map/pair_lists/pallas_call | solution.py:134
  75.3 7.2 %collective-permute-start.9 = (f32[12,128,128]{2,1,0:T(8,128)}, f32[12,128,128]{2,1,0:T(8,128)S(1)}, u32[]{:S(2)}, u32[]{:S(2)}) collective-permute-start(f32[12,128,128]{2,1,0:T(8,128)} %collective-permute-done.5.b2), channel_id=1, source_target_pairs={{1,0},{2,1},{3,2},{4,3},{5,4},{6,5},{7,6},{8,7},{9,8},{10,9},{11,1... | collective-permute-start | bytes 2359304 | tf_op jit(solution)/shard_map/ppermute | solution.py:31
  82.5 0.7 copy-done
  83.9 16.2 %near_step.1 = (f32[64,128,128]{2,1,0:T(8,128)}, f32[128,128,128]{2,1,0:T(8,128)}, f32[96,128,128]{2,1,0:T(8,128)}, bf16[97,128,256]{2,1,0:T(8,128)(2,1)}) custom-call(s32[5472]{0:T(1024)S(1)} %copy-done, s32[6]{0:T(128)S(1)} %copy-done.2, s32[96]{0:T(128)S(1)} %select_n.145.carry, f32[12,128,128]{2,1,0:T(8,128)S(1)} %collective-permute-done.4.b1, ...), custom_call_target="tpu_custom_call" | custom-call | flops 10000000000 | bytes 30000000 | tf_op jit(solution)/shard_map/near_step/pallas_call | solution.py:310
  100.1 11.5 %middle_step.1 = (f32[64,128,128]{2,1,0:T(8,128)S(1)}, f32[96,128,128]{2,1,0:T(8,128)S(1)}) custom-call(s32[5472]{0:T(1024)S(1)} %copy-done.1, s32[6]{0:T(128)S(1)} %copy-done.2, f32[20,128,128]{2,1,0:T(8,128)} %collective-permute-done.10.below.refs_0_, f32[20,128,128]{2,1,0:T(8,128)} %collective-permute-done.11.above.refs_1_, ...), custom_call_target="tpu_custom_call" | custom-call | flops 10000000000 | bytes 40000000 | tf_op jit(solution)/shard_map/middle_step/pallas_call | solution.py:335
  112.1 7.2 %last_step.1 = f32[96,128,128]{2,1,0:T(8,128)} custom-call(s32[5472]{0:T(1024)S(1)} %copy-done.1, s32[6]{0:T(128)S(1)} %copy-done.2, f32[12,128,128]{2,1,0:T(8,128)S(1)} %collective-permute-done.8.below, f32[12,128,128]{2,1,0:T(8,128)S(1)} %collective-permute-done.9.above, bf16[97,128,256]{2,1,0:T(8,128)(2,1)} %get-tuple-element.57.left_in, ...), custom_call_target="tpu_custom_call" | custom-call | flops 10000000000 | bytes 40000000 | tf_op jit(solution)/shard_map/last_step/pallas_call | solution.py:335
  (104 shorter events, 8.1 us)
Async XLA Ops:
  0.6 51.8 %copy-start.3 = (pred[8,8]{1,0:T(8,128)(4,1)S(1)}, pred[8,8]{1,0:T(8,128)(4,1)}, u32[]{:S(2)}) copy-start(pred[8,8]{1,0:T(8,128)(4,1)} %constant.152) | copy-start | bytes 196
  1.4 14.0 %collective-permute-start.3 = (s32[4,24]{1,0:T(4,128)S(1)}, s32[4,24]{1,0:T(4,128)S(1)}, u32[]{:S(2)}, u32[]{:S(2)}) collective-permute-start(s32[4,24]{1,0:T(4,128)S(1)} %pad_add_fusion.4), channel_id=1, source_target_pairs={{2,0},{3,1},{4,2},{5,3},{6,4},{7,5},{8,6},{9,7},{10,8},{11,9},{12,... | collective-permute-start | bytes 1160 | tf_op jit(solution)/shard_map/ppermute | solution.py:31
  9.8 12.8 %collective-permute-start.2 = (s32[4,24]{1,0:T(4,128)S(1)}, s32[4,24]{1,0:T(4,128)S(1)}, u32[]{:S(2)}, u32[]{:S(2)}) collective-permute-start(s32[4,24]{1,0:T(4,128)S(1)} %pad_add_fusion.4), channel_id=1, source_target_pairs={{1,0},{2,1},{3,2},{4,3},{5,4},{6,5},{7,6},{8,7},{9,8},{10,9},{11,1... | collective-permute-start | bytes 1160 | tf_op jit(solution)/shard_map/ppermute | solution.py:31
  10.6 12.0 %collective-permute-start.1 = (s32[4,24]{1,0:T(4,128)S(1)}, s32[4,24]{1,0:T(4,128)S(1)}, u32[]{:S(2)}, u32[]{:S(2)}) collective-permute-start(s32[4,24]{1,0:T(4,128)S(1)} %pad_add_fusion.4), channel_id=1, source_target_pairs={{255,0},{0,1},{1,2},{2,3},{3,4},{4,5},{5,6},{6,7},{7,8},{8,9},{9,1... | collective-permute-start | bytes 1160 | tf_op jit(solution)/shard_map/ppermute | solution.py:31
  11.8 10.8 %collective-permute-start = (s32[4,24]{1,0:T(4,128)S(1)}, s32[4,24]{1,0:T(4,128)S(1)}, u32[]{:S(2)}, u32[]{:S(2)}) collective-permute-start(s32[4,24]{1,0:T(4,128)S(1)} %pad_add_fusion.4), channel_id=1, source_target_pairs={{254,0},{255,1},{0,2},{1,3},{2,4},{3,5},{4,6},{5,7},{6,8},{7,9},{8... | collective-permute-start | bytes 1160 | tf_op jit(solution)/shard_map/ppermute | solution.py:31
  15.2 40.1 %collective-permute-start.6 = (f32[20,128,128]{2,1,0:T(8,128)}, f32[20,128,128]{2,1,0:T(8,128)S(1)}, u32[]{:S(2)}, u32[]{:S(2)}) collective-permute-start(f32[20,128,128]{2,1,0:T(8,128)} %get-tuple-element.35), channel_id=1, source_target_pairs={{255,0},{0,1},{1,2},{2,3},{3,4},{4,5},{5,6},{6,7},{7,8},{8,9},{9,1... | collective-permute-start | bytes 3932168 | tf_op jit(solution)/shard_map/ppermute | solution.py:31
  15.4 39.9 %collective-permute-start.7 = (f32[20,128,128]{2,1,0:T(8,128)}, f32[20,128,128]{2,1,0:T(8,128)S(1)}, u32[]{:S(2)}, u32[]{:S(2)}) collective-permute-start(f32[20,128,128]{2,1,0:T(8,128)} %get-tuple-element.36), channel_id=1, source_target_pairs={{1,0},{2,1},{3,2},{4,3},{5,4},{6,5},{7,6},{8,7},{9,8},{10,9},{11,1... | collective-permute-start | bytes 3932168 | tf_op jit(solution)/shard_map/ppermute | solution.py:31
  44.4 30.8 %collective-permute-start.4 = (f32[12,128,128]{2,1,0:T(8,128)}, f32[12,128,128]{2,1,0:T(8,128)S(1)}, u32[]{:S(2)}, u32[]{:S(2)}) collective-permute-start(f32[12,128,128]{2,1,0:T(8,128)} %get-tuple-element.33), channel_id=1, source_target_pairs={{255,0},{0,1},{1,2},{2,3},{3,4},{4,5},{5,6},{6,7},{7,8},{8,9},{9,1... | collective-permute-start | bytes 2359304 | tf_op jit(solution)/shard_map/ppermute | solution.py:31
  44.5 30.7 %collective-permute-start.5 = (f32[12,128,128]{2,1,0:T(8,128)}, f32[12,128,128]{2,1,0:T(8,128)}, u32[]{:S(2)}, u32[]{:S(2)}) collective-permute-start(f32[12,128,128]{2,1,0:T(8,128)} %get-tuple-element.34), channel_id=1, source_target_pairs={{1,0},{2,1},{3,2},{4,3},{5,4},{6,5},{7,6},{8,7},{9,8},{10,9},{11,1... | collective-permute-start | bytes 2359304 | tf_op jit(solution)/shard_map/ppermute | solution.py:31
  55.3 44.8 %collective-permute-start.10 = (f32[20,128,128]{2,1,0:T(8,128)S(1)}, f32[20,128,128]{2,1,0:T(8,128)}, u32[]{:S(2)}, u32[]{:S(2)}) collective-permute-start(f32[20,128,128]{2,1,0:T(8,128)S(1)} %collective-permute-done.6.a1), channel_id=1, source_target_pairs={{255,0},{0,1},{1,2},{2,3},{3,4},{4,5},{5,6},{6,7},{7,8},{8,9},{9,1... | collective-permute-start | bytes 3932168 | tf_op jit(solution)/shard_map/ppermute | solution.py:31
  55.3 44.8 %collective-permute-start.11 = (f32[20,128,128]{2,1,0:T(8,128)S(1)}, f32[20,128,128]{2,1,0:T(8,128)}, u32[]{:S(2)}, u32[]{:S(2)}) collective-permute-start(f32[20,128,128]{2,1,0:T(8,128)S(1)} %collective-permute-done.7.a2), channel_id=1, source_target_pairs={{1,0},{2,1},{3,2},{4,3},{5,4},{6,5},{7,6},{8,7},{9,8},{10,9},{11,1... | collective-permute-start | bytes 3932168 | tf_op jit(solution)/shard_map/ppermute | solution.py:31
  75.2 36.9 %collective-permute-start.8 = (f32[12,128,128]{2,1,0:T(8,128)S(1)}, f32[12,128,128]{2,1,0:T(8,128)S(1)}, u32[]{:S(2)}, u32[]{:S(2)}) collective-permute-start(f32[12,128,128]{2,1,0:T(8,128)S(1)} %collective-permute-done.4.b1), channel_id=1, source_target_pairs={{255,0},{0,1},{1,2},{2,3},{3,4},{4,5},{5,6},{6,7},{7,8},{8,9},{9,1... | collective-permute-start | bytes 2359304 | tf_op jit(solution)/shard_map/ppermute | solution.py:31
  75.3 36.8 %collective-permute-start.9 = (f32[12,128,128]{2,1,0:T(8,128)}, f32[12,128,128]{2,1,0:T(8,128)S(1)}, u32[]{:S(2)}, u32[]{:S(2)}) collective-permute-start(f32[12,128,128]{2,1,0:T(8,128)} %collective-permute-done.5.b2), channel_id=1, source_target_pairs={{1,0},{2,1},{3,2},{4,3},{5,4},{6,5},{7,6},{8,7},{9,8},{10,9},{11,1... | collective-permute-start | bytes 2359304 | tf_op jit(solution)/shard_map/ppermute | solution.py:31
  82.5 0.7 copy-start
  83.2 0.7 copy-start.2
  83.9 16.2 %copy-start.1 = (s32[5472]{0:T(1024)S(1)}, s32[5472]{0:T(1024)}, u32[]{:S(2)}) copy-start(s32[5472]{0:T(1024)} %get-tuple-element.49.lists) | copy-start | bytes 65668

commit v5 on v4

--- a/solution.py
+++ b/solution.py
@@ -22,8 +22,9 @@
 
 TARGETS = (12 * KS, 4 * KC, 8 * KS, 4 * KC, 4 * KS, 4 * KC)
 ZERO_RIGHT = (12 * KP, 4 * KS, 2 * PIECE, 4 * KS, 2 * PIECE, 4 * KS)
+SPARE = (0, 0, 0, 0, 0, 4 * KC)
 TABLE_OFF = tuple(int(x) for x in np.cumsum((0,) + tuple(t * KP for t in TARGETS)))
-LIST_OFF = tuple(int(x) for x in np.cumsum((0,) + tuple(t * KP + GROUP for t in TARGETS)))
+LIST_OFF = tuple(int(x) for x in np.cumsum((0,) + tuple(t * KP + 2 * GROUP for t in TARGETS)))
 
 
 def shifted(x, distance):
@@ -123,7 +124,7 @@
 
         n = lax.fori_loop(0, TARGETS[which] // 4, targets, jnp.int32(0))
         start += TARGETS[which]
-        filler = ZERO_LEFT | (ZERO_RIGHT[which] << 8)
+        filler = ZERO_LEFT | (ZERO_RIGHT[which] << 8) | (SPARE[which] << 16)
         for q in range(GROUP):
             lists[l0 + n + q] = filler
         counts[which] = (n + GROUP - 1) // GROUP
@@ -165,22 +166,26 @@
     lax.fori_loop(0, (hi - lo) // step, many, 0)
 
 
-def multiply(which, lists, counts, left, right, total, scale=None):
+def multiply(which, lists, counts, left, right, total):
     def group(g, _):
-        at = LIST_OFF[which] + g * GROUP
-        none = jnp.zeros((BS, BS), jnp.bfloat16)
-        done = []
-        for x in range(GROUP):
-            e = lists[at + x]
-            b = right[(e >> 8) & 255]
-            rhs = jnp.concatenate([b, jnp.concatenate([b[:, :BS], none], axis=1)], axis=0)
-            r = jnp.dot(left[e & 255], rhs, preferred_element_type=jnp.float32)
-            done.append((e >> 16, r[:, :BS] + r[:, BS:]))
-        for t, q in done:
-            total[t] = total[t] + (q if scale is None else scale * q)
+        multiply_group(which, g, lists, left, right, total)
         return 0
 
     lax.fori_loop(0, counts[which], group, 0)
+
+
+def multiply_group(which, g, lists, left, right, total):
+    at = LIST_OFF[which] + g * GROUP
+    none = jnp.zeros((BS, BS), jnp.bfloat16)
+    done = []
+    for x in range(GROUP):
+        e = lists[at + x]
+        b = right[(e >> 8) & 255]
+        rhs = jnp.concatenate([b, jnp.concatenate([b[:, :BS], none], axis=1)], axis=0)
+        r = jnp.dot(left[e & 255], rhs, preferred_element_type=jnp.float32)
+        done.append((e >> 16, r[:, :BS] + r[:, BS:]))
+    for t, q in done:
+        total[t] = total[t] + q
 
 
 def zero(ref, at):
@@ -257,7 +262,7 @@
         loads.append(pltpu.make_async_copy(left_in.at[pl.ds(at, n)], left.at[pl.ds(at, n)], sems.at[2 + i]))
     own_left = loads.pop()
     loads.append(pltpu.make_async_copy(sp_in, sp, sems.at[5]))
-    c_copy = pltpu.make_async_copy(c_in, c, sems.at[6])
+    c_copy = pltpu.make_async_copy(c_in, c.at[pl.ds(0, 4 * KC)], sems.at[6])
     for copy in loads + [own_left, c_copy]:
         copy.start()
     zero(right, 2 * PIECE)
@@ -275,17 +280,37 @@
     each(0, 4 * KS, lambda q: put(s_cut, q, sp[q]))
     own_left.wait()
     c_copy.wait()
-    multiply(which + 1, lists, counts, left, s_cut, c, scale=-2.0 if final else None)
-    for i in range(ROWS):
-        if not final:
+    if final:
+
+        def row_copy(i):
+            piece = pl.ds(i * KC, KC)
+            return pltpu.make_async_copy(c.at[piece], out.at[piece], sems.at[8 + i])
+
+        def row(i, g):
+            def here(g):
+                first = lists[LIST_OFF[5] + jnp.minimum(g, counts[5]) * GROUP] >> 16
+                return jnp.logical_and(g < counts[5], first < (i + 1) * KC)
+
+            def step(g):
+                multiply_group(5, g, lists, left, s_cut, c)
+                return g + 1
+
+            g = lax.while_loop(here, step, g)
 
             def finish(q):
-                c[q] = -2.0 * c[q]
-
-            each(i * KC, (i + 1) * KC, finish)
-        piece = pl.ds(i * KC, KC)
-        done.append(pltpu.make_async_copy(c.at[piece], out.at[piece], sems.at[8 + i]))
-        done[-1].start()
+                c[i * KC + q] = -2.0 * c[i * KC + q]
+
+            each(0, KC, finish)
+            row_copy(i).start()
+            return g
+
+        lax.fori_loop(0, ROWS, row, jnp.int32(0))
+        for i in range(ROWS):
+            row_copy(i).wait()
+        return
+    multiply(which + 1, lists, counts, left, s_cut, c)
+    done.append(pltpu.make_async_copy(c.at[pl.ds(0, 4 * KC)], out, sems.at[8]))
+    done[-1].start()
     for copy in done:
         copy.wait()
 
@@ -343,7 +368,7 @@
             vmem_cut(2 * PIECE),
             vmem_f32((4 if final else 8) * KS),
             vmem_cut(4 * KS),
-            vmem_f32(4 * KC),
+            vmem_f32(4 * KC + 1),
             pltpu.SemaphoreType.DMA((16,)),
         ],
         compiler_params=pltpu.CompilerParams(vmem_limit_bytes=36 * 1024 * 1024),

time: 121 us -> 121 us (level)
  no operation moved by 1% of the time
where the time goes in v5:
time: 121 us; the launch traced here: 119 us
  Pallas kernels  52.2 us (43%)
  starting transfers between devices  40.1 us (33%)
  other arithmetic  19.3 us (16%)
  local copies, waits for them, and re-layouts  5.74 us (5%)
  between operations  1.33 us (1%)
    ppermute x12, starting transfers between devices, shifted(): return lax.ppermute(x, AXES, [((i - distance) % n, i) for i in range(n)])  40.1 us
    pallas_call x2, Pallas kernels, far_step(): pl.pallas_call(functools.partial(far_kernel, final), out_shape=f32(4 * KC...  18 us
    pallas_call x1, Pallas kernels, near_step(): pl.pallas_call(near_kernel, out_shape=(f32(4 * KS), f32(8 * KS), f32(4 *...  16.6 us
    pallas_call x1, Pallas kernels, pair_lists(): pl.pallas_call(list_kernel, out_shape=(jax.ShapeDtypeStruct((LIST_OFF[-1]...  12.7 us
    reduce_sum x6, other arithmetic, pick(): return jnp.sum(jnp.where(hot.reshape(shape), table, 0), axis=index.ndim)  5.66 us
    pallas_call x2, Pallas kernels, split(): pl.pallas_call(functools.partial(split_kernel, ranges), out_shape=tuple((...  4.86 us
    or x8, other arithmetic, entries(): left[:, None, :] | right << 8 | target[:, :, None] << 16  3.09 us
  transfers between devices with their start and end apart: 12, of which 1 were waited for; matrix products, arithmetic and copies ran while one was open for 19% of the time, Pallas kernels for 38%

profile of v5, /device:TPU:0, one launch (start us, length us, event | category | flops | bytes accessed | tf_op | source)
XLA Modules:
  0.0 119.3 jit_solution(9379316619789119071)
XLA Ops:
  0.6 0.8 pad_add_fusion.4
  1.4 8.4 %collective-permute-start.3 = (s32[4,24]{1,0:T(4,128)S(1)}, s32[4,24]{1,0:T(4,128)S(1)}, u32[]{:S(2)}, u32[]{:S(2)}) collective-permute-start(s32[4,24]{1,0:T(4,128)S(1)} %pad_add_fusion.4), channel_id=1, source_target_pairs={{2,0},{3,1},{4,2},{5,3},{6,4},{7,5},{8,6},{9,7},{10,8},{11,9},{12,... | collective-permute-start | bytes 1160 | tf_op jit(solution)/shard_map/ppermute | solution.py:32
  9.8 0.8 collective-permute-start.2
  10.6 1.3 %collective-permute-start.1 = (s32[4,24]{1,0:T(4,128)S(1)}, s32[4,24]{1,0:T(4,128)S(1)}, u32[]{:S(2)}, u32[]{:S(2)}) collective-permute-start(s32[4,24]{1,0:T(4,128)S(1)} %pad_add_fusion.4), channel_id=1, source_target_pairs={{255,0},{0,1},{1,2},{2,3},{3,4},{4,5},{5,6},{6,7},{7,8},{8,9},{9,1... | collective-permute-start | bytes 1160 | tf_op jit(solution)/shard_map/ppermute | solution.py:32
  12.6 2.6 %split.3 = (f32[20,128,128]{2,1,0:T(8,128)}, f32[20,128,128]{2,1,0:T(8,128)}) custom-call(f32[32,128,128]{2,1,0:T(8,128)} %bitcast.28), custom_call_target="tpu_custom_call" | custom-call | bytes 4000000 | tf_op jit(solution)/shard_map/split/pallas_call | solution.py:399
  15.4 7.2 %collective-permute-start.7 = (f32[20,128,128]{2,1,0:T(8,128)}, f32[20,128,128]{2,1,0:T(8,128)S(1)}, u32[]{:S(2)}, u32[]{:S(2)}) collective-permute-start(f32[20,128,128]{2,1,0:T(8,128)} %get-tuple-element.36), channel_id=1, source_target_pairs={{1,0},{2,1},{3,2},{4,3},{5,4},{6,5},{7,6},{8,7},{9,8},{10,9},{11,1... | collective-permute-start | bytes 3932168 | tf_op jit(solution)/shard_map/ppermute | solution.py:32
  24.0 1.0 fusion.7
  25.1 0.8 pad_add_fusion.5
  25.9 0.8 pad_add_fusion.2
  26.8 0.9 select_reduce_fusion.9
  27.7 0.9 select_reduce_fusion.8
  28.8 1.0 select_reduce_fusion.6
  30.6 0.8 select_reduce_fusion.7
  31.8 1.7 %compare_reduce_fusion = pred[4,12,16]{2,1,0:T(8,128)(4,1)S(1)} fusion(s32[4,24]{1,0:T(4,128)} %param.26, s32[12,16]{1,0:T(8,128)S(1)} %slice.121), kind=kLoop, calls=%fused_computation.2 | loop fusion | flops 36096 | bytes 1920 | tf_op jit(solution)/shard_map/reduce_or | solution.py:74
  33.6 0.9 select_reduce_fusion.2
  35.0 0.8 shift-left_or_fusion.2
  36.1 0.7 broadcast_or_fusion
  36.9 1.7 %select_reduce_fusion.1 = s32[12,8,8]{2,1,0:T(8,128)S(1)} fusion(s32[20,8]{0,1:T(8,128)S(1)} %copy.56, pred[12,8,20]{2,1,0:T(8,128)(4,1)S(1)} %iota_compare_fusion.2), kind=kLoop, calls=%fused_computation.1 | loop fusion | flops 29952 | bytes 5632 | tf_op jit(solution)/shard_map/reduce_sum | solution.py:53
  39.5 0.8 shift-left_or_fusion.3
  40.4 0.8 shift-left_or_fusion.1
  41.3 0.8 shift-left_or_fusion
  42.2 2.2 %split.2 = (f32[12,128,128]{2,1,0:T(8,128)}, f32[12,128,128]{2,1,0:T(8,128)}) custom-call(f32[32,128,128]{2,1,0:T(8,128)} %bitcast.29), custom_call_target="tpu_custom_call" | custom-call | bytes 4000000 | tf_op jit(solution)/shard_map/split/pallas_call | solution.py:399
  44.5 7.2 %collective-permute-start.5 = (f32[12,128,128]{2,1,0:T(8,128)}, f32[12,128,128]{2,1,0:T(8,128)}, u32[]{:S(2)}, u32[]{:S(2)}) collective-permute-start(f32[12,128,128]{2,1,0:T(8,128)} %get-tuple-element.34), channel_id=1, source_target_pairs={{1,0},{2,1},{3,2},{4,3},{5,4},{6,5},{7,6},{8,7},{9,8},{10,9},{11,1... | collective-permute-start | bytes 2359304 | tf_op jit(solution)/shard_map/ppermute | solution.py:32
  52.6 0.9 copy.70
  53.5 1.8 %reshape.321.table = s32[5376]{0:T(1024)} reshape(s32[672,8]{1,0:T(8,128)} %copy.70) | data formatting | bytes 43008 | tf_op jit(solution)/shard_map/reshape | solution.py:99
  55.3 7.2 %collective-permute-start.11 = (f32[20,128,128]{2,1,0:T(8,128)S(1)}, f32[20,128,128]{2,1,0:T(8,128)}, u32[]{:S(2)}, u32[]{:S(2)}) collective-permute-start(f32[20,128,128]{2,1,0:T(8,128)S(1)} %collective-permute-done.7.a2), channel_id=1, source_target_pairs={{1,0},{2,1},{3,2},{4,3},{5,4},{6,5},{7,6},{8,7},{9,8},{10,9},{11,1... | collective-permute-start | bytes 3932168 | tf_op jit(solution)/shard_map/ppermute | solution.py:32
  62.5 12.7 %pair_lists.1 = (s32[5568]{0:T(1024)}, s32[6]{0:T(128)}) custom-call(s32[5376]{0:T(1024)} %reshape.321.table, s32[672]{0:T(1024)} %get-tuple-element.45.hits), custom_call_target="tpu_custom_call" | custom-call | flops 20000000 | bytes 40000000 | tf_op jit(solution)/shard_map/pair_lists/pallas_call | solution.py:135
  75.3 7.2 %collective-permute-start.9 = (f32[12,128,128]{2,1,0:T(8,128)}, f32[12,128,128]{2,1,0:T(8,128)S(1)}, u32[]{:S(2)}, u32[]{:S(2)}) collective-permute-start(f32[12,128,128]{2,1,0:T(8,128)} %collective-permute-done.5.b2), channel_id=1, source_target_pairs={{1,0},{2,1},{3,2},{4,3},{5,4},{6,5},{7,6},{8,7},{9,8},{10,9},{11,1... | collective-permute-start | bytes 2359304 | tf_op jit(solution)/shard_map/ppermute | solution.py:32
  82.5 0.7 copy-done
  83.9 16.6 %near_step.1 = (f32[64,128,128]{2,1,0:T(8,128)}, f32[128,128,128]{2,1,0:T(8,128)}, f32[96,128,128]{2,1,0:T(8,128)}, bf16[97,128,256]{2,1,0:T(8,128)(2,1)}) custom-call(s32[5568]{0:T(1024)S(1)} %copy-done, s32[6]{0:T(128)S(1)} %copy-done.2, s32[96]{0:T(128)S(1)} %select_n.145.carry, f32[12,128,128]{2,1,0:T(8,128)S(1)} %collective-permute-done.4.b1, ...), custom_call_target="tpu_custom_call" | custom-call | flops 10000000000 | bytes 30000000 | tf_op jit(solution)/shard_map/near_step/pallas_call | solution.py:335
  100.5 11.0 %middle_step.1 = (f32[64,128,128]{2,1,0:T(8,128)S(1)}, f32[96,128,128]{2,1,0:T(8,128)S(1)}) custom-call(s32[5568]{0:T(1024)S(1)} %copy-done.1, s32[6]{0:T(128)S(1)} %copy-done.2, f32[20,128,128]{2,1,0:T(8,128)} %collective-permute-done.10.below.refs_0_, f32[20,128,128]{2,1,0:T(8,128)} %collective-permute-done.11.above.refs_1_, ...), custom_call_target="tpu_custom_call" | custom-call | flops 10000000000 | bytes 40000000 | tf_op jit(solution)/shard_map/middle_step/pallas_call | solution.py:360
  112.1 7.0 %last_step.1 = f32[96,128,128]{2,1,0:T(8,128)} custom-call(s32[5568]{0:T(1024)S(1)} %copy-done.1, s32[6]{0:T(128)S(1)} %copy-done.2, f32[12,128,128]{2,1,0:T(8,128)S(1)} %collective-permute-done.8.below, f32[12,128,128]{2,1,0:T(8,128)S(1)} %collective-permute-done.9.above, bf16[97,128,256]{2,1,0:T(8,128)(2,1)} %get-tuple-element.57.left_in, ...), custom_call_target="tpu_custom_call" | custom-call | flops 10000000000 | bytes 40000000 | tf_op jit(solution)/shard_map/last_step/pallas_call | solution.py:360
  (104 shorter events, 8.2 us)
Async XLA Ops:
  0.6 51.8 %copy-start.3 = (pred[8,8]{1,0:T(8,128)(4,1)S(1)}, pred[8,8]{1,0:T(8,128)(4,1)}, u32[]{:S(2)}) copy-start(pred[8,8]{1,0:T(8,128)(4,1)} %constant.152) | copy-start | bytes 196
  1.4 14.0 %collective-permute-start.3 = (s32[4,24]{1,0:T(4,128)S(1)}, s32[4,24]{1,0:T(4,128)S(1)}, u32[]{:S(2)}, u32[]{:S(2)}) collective-permute-start(s32[4,24]{1,0:T(4,128)S(1)} %pad_add_fusion.4), channel_id=1, source_target_pairs={{2,0},{3,1},{4,2},{5,3},{6,4},{7,5},{8,6},{9,7},{10,8},{11,9},{12,... | collective-permute-start | bytes 1160 | tf_op jit(solution)/shard_map/ppermute | solution.py:32
  9.8 12.8 %collective-permute-start.2 = (s32[4,24]{1,0:T(4,128)S(1)}, s32[4,24]{1,0:T(4,128)S(1)}, u32[]{:S(2)}, u32[]{:S(2)}) collective-permute-start(s32[4,24]{1,0:T(4,128)S(1)} %pad_add_fusion.4), channel_id=1, source_target_pairs={{1,0},{2,1},{3,2},{4,3},{5,4},{6,5},{7,6},{8,7},{9,8},{10,9},{11,1... | collective-permute-start | bytes 1160 | tf_op jit(solution)/shard_map/ppermute | solution.py:32
  10.6 12.0 %collective-permute-start.1 = (s32[4,24]{1,0:T(4,128)S(1)}, s32[4,24]{1,0:T(4,128)S(1)}, u32[]{:S(2)}, u32[]{:S(2)}) collective-permute-start(s32[4,24]{1,0:T(4,128)S(1)} %pad_add_fusion.4), channel_id=1, source_target_pairs={{255,0},{0,1},{1,2},{2,3},{3,4},{4,5},{5,6},{6,7},{7,8},{8,9},{9,1... | collective-permute-start | bytes 1160 | tf_op jit(solution)/shard_map/ppermute | solution.py:32
  11.8 10.8 %collective-permute-start = (s32[4,24]{1,0:T(4,128)S(1)}, s32[4,24]{1,0:T(4,128)S(1)}, u32[]{:S(2)}, u32[]{:S(2)}) collective-permute-start(s32[4,24]{1,0:T(4,128)S(1)} %pad_add_fusion.4), channel_id=1, source_target_pairs={{254,0},{255,1},{0,2},{1,3},{2,4},{3,5},{4,6},{5,7},{6,8},{7,9},{8... | collective-permute-start | bytes 1160 | tf_op jit(solution)/shard_map/ppermute | solution.py:32
  15.2 40.1 %collective-permute-start.6 = (f32[20,128,128]{2,1,0:T(8,128)}, f32[20,128,128]{2,1,0:T(8,128)S(1)}, u32[]{:S(2)}, u32[]{:S(2)}) collective-permute-start(f32[20,128,128]{2,1,0:T(8,128)} %get-tuple-element.35), channel_id=1, source_target_pairs={{255,0},{0,1},{1,2},{2,3},{3,4},{4,5},{5,6},{6,7},{7,8},{8,9},{9,1... | collective-permute-start | bytes 3932168 | tf_op jit(solution)/shard_map/ppermute | solution.py:32
  15.4 39.9 %collective-permute-start.7 = (f32[20,128,128]{2,1,0:T(8,128)}, f32[20,128,128]{2,1,0:T(8,128)S(1)}, u32[]{:S(2)}, u32[]{:S(2)}) collective-permute-start(f32[20,128,128]{2,1,0:T(8,128)} %get-tuple-element.36), channel_id=1, source_target_pairs={{1,0},{2,1},{3,2},{4,3},{5,4},{6,5},{7,6},{8,7},{9,8},{10,9},{11,1... | collective-permute-start | bytes 3932168 | tf_op jit(solution)/shard_map/ppermute | solution.py:32
  44.4 30.8 %collective-permute-start.4 = (f32[12,128,128]{2,1,0:T(8,128)}, f32[12,128,128]{2,1,0:T(8,128)S(1)}, u32[]{:S(2)}, u32[]{:S(2)}) collective-permute-start(f32[12,128,128]{2,1,0:T(8,128)} %get-tuple-element.33), channel_id=1, source_target_pairs={{255,0},{0,1},{1,2},{2,3},{3,4},{4,5},{5,6},{6,7},{7,8},{8,9},{9,1... | collective-permute-start | bytes 2359304 | tf_op jit(solution)/shard_map/ppermute | solution.py:32
  44.5 30.7 %collective-permute-start.5 = (f32[12,128,128]{2,1,0:T(8,128)}, f32[12,128,128]{2,1,0:T(8,128)}, u32[]{:S(2)}, u32[]{:S(2)}) collective-permute-start(f32[12,128,128]{2,1,0:T(8,128)} %get-tuple-element.34), channel_id=1, source_target_pairs={{1,0},{2,1},{3,2},{4,3},{5,4},{6,5},{7,6},{8,7},{9,8},{10,9},{11,1... | collective-permute-start | bytes 2359304 | tf_op jit(solution)/shard_map/ppermute | solution.py:32
  55.3 45.2 %collective-permute-start.10 = (f32[20,128,128]{2,1,0:T(8,128)S(1)}, f32[20,128,128]{2,1,0:T(8,128)}, u32[]{:S(2)}, u32[]{:S(2)}) collective-permute-start(f32[20,128,128]{2,1,0:T(8,128)S(1)} %collective-permute-done.6.a1), channel_id=1, source_target_pairs={{255,0},{0,1},{1,2},{2,3},{3,4},{4,5},{5,6},{6,7},{7,8},{8,9},{9,1... | collective-permute-start | bytes 3932168 | tf_op jit(solution)/shard_map/ppermute | solution.py:32
  55.3 45.2 %collective-permute-start.11 = (f32[20,128,128]{2,1,0:T(8,128)S(1)}, f32[20,128,128]{2,1,0:T(8,128)}, u32[]{:S(2)}, u32[]{:S(2)}) collective-permute-start(f32[20,128,128]{2,1,0:T(8,128)S(1)} %collective-permute-done.7.a2), channel_id=1, source_target_pairs={{1,0},{2,1},{3,2},{4,3},{5,4},{6,5},{7,6},{8,7},{9,8},{10,9},{11,1... | collective-permute-start | bytes 3932168 | tf_op jit(solution)/shard_map/ppermute | solution.py:32
  75.2 36.9 %collective-permute-start.8 = (f32[12,128,128]{2,1,0:T(8,128)S(1)}, f32[12,128,128]{2,1,0:T(8,128)S(1)}, u32[]{:S(2)}, u32[]{:S(2)}) collective-permute-start(f32[12,128,128]{2,1,0:T(8,128)S(1)} %collective-permute-done.4.b1), channel_id=1, source_target_pairs={{255,0},{0,1},{1,2},{2,3},{3,4},{4,5},{5,6},{6,7},{7,8},{8,9},{9,1... | collective-permute-start | bytes 2359304 | tf_op jit(solution)/shard_map/ppermute | solution.py:32
  75.3 36.8 %collective-permute-start.9 = (f32[12,128,128]{2,1,0:T(8,128)}, f32[12,128,128]{2,1,0:T(8,128)S(1)}, u32[]{:S(2)}, u32[]{:S(2)}) collective-permute-start(f32[12,128,128]{2,1,0:T(8,128)} %collective-permute-done.5.b2), channel_id=1, source_target_pairs={{1,0},{2,1},{3,2},{4,3},{5,4},{6,5},{7,6},{8,7},{9,8},{10,9},{11,1... | collective-permute-start | bytes 2359304 | tf_op jit(solution)/shard_map/ppermute | solution.py:32
  82.5 0.7 copy-start
  83.2 0.7 copy-start.2
  83.9 16.7 %copy-start.1 = (s32[5568]{0:T(1024)S(1)}, s32[5568]{0:T(1024)}, u32[]{:S(2)}) copy-start(s32[5568]{0:T(1024)} %get-tuple-element.49.lists) | copy-start | bytes 66820
